TPU v7x, 512 devices: a whole 4x8x8 slice. The times are simulated.
512 devices in a mesh: rep: 32 (over y, z_hi), shard: 16 (over z_lo, x, core).
Axes of the slice: x: 4, y: 8, z: 8 (z_hi: 4, z_lo: 2; z = z_hi * 2 + z_lo), core: 2. Of those that a mesh axis runs over, the one named last changes fastest.
Arguments:
- grad: bfloat16 [8192, 2048], P('shard'), may hold values from -1.5 to 1.5
- owner: int32 [32, 8], replicated, may hold values from 0 to 15, as said below
- left_basis: bfloat16 [256, 256, 256], P('shard', 'rep'), may hold values from -0.375 to 0.375
- right_basis: bfloat16 [256, 256, 256], P('shard', 'rep'), may hold values from -0.375 to 0.375
- avg: bfloat16 [256, 256, 256], P('shard', 'rep'), may hold values from -1.5 to 1.5
- avg_sq: float32 [256, 256, 256], P('shard', 'rep'), may hold values from 0.002 to 0.1
- left_gram: float32 [256, 256, 256], P('shard', 'rep'), may hold values from -6 to 6
- right_gram: float32 [256, 256, 256], P('shard', 'rep'), may hold values from -6 to 6
Outputs:
- update: bfloat16 [8192, 2048], P('shard')
- new_avg: bfloat16 [256, 256, 256], P('shard', 'rep')
- new_avg_sq: float32 [256, 256, 256], P('shard', 'rep')
- new_left_gram: float32 [256, 256, 256], P('shard', 'rep')
- new_right_gram: float32 [256, 256, 256], P('shard', 'rep')
Inputs may be any that keep to these rules, and one draw needn't show every extreme that they name: Each shard owns exactly 16 blocks; of the 16 blocks in one shard's rows, at most 2 share an owner, and in every shard's rows exactly 2 blocks share one owner.
All inputs are finite; a program needn't handle non-finite values.
Results may differ from a plain program's by a relative error of at most 0.0059.
Values may be sent and summed in bfloat16 or wider, within the bound.
A program may use at most 64 MiB of HBM per device.

v0:
```python
import jax
import jax.numpy as jnp
from jax import lax
from jax.sharding import PartitionSpec as P

CAP = 2


BETA_ONE = 0.9
BETA_TWO = 0.95
EPSILON = 1e-08


def owner_ranks(flat, shards):
    hits = (flat[:, None] == jnp.arange(shards, dtype=jnp.int32)[None, :]).astype(jnp.int32)
    return jnp.sum((jnp.cumsum(hits, axis=0) - hits) * hits, axis=1)


def pick_index(targets, width):
    slots = jnp.arange(width, dtype=jnp.int32)
    match = (targets[None, :] == slots[:, None]).astype(jnp.int32)
    places = jnp.arange(targets.shape[0], dtype=jnp.int32)
    return (jnp.sum(match * places[None, :], axis=1), jnp.sum(match, axis=1) > 0)


def body(grad, owner, left_basis, right_basis, avg, avg_sq, left_gram, right_gram):
    shards = lax.axis_size("shard")
    here = lax.axis_index("shard")
    there = lax.axis_index("rep")
    kept, slice_rows, width = left_basis.shape
    row_blocks = grad.shape[0] // width
    col_blocks = grad.shape[1] // width
    per_shard = row_blocks * col_blocks
    flat = owner.reshape(-1)
    total = flat.shape[0]
    ident = jnp.arange(total, dtype=jnp.int32)
    source = ident // per_shard
    ranks = owner_ranks(flat, shards)
    pair_key = source * shards + flat
    earlier = (pair_key[:, None] == pair_key[None, :]) & (ident[None, :] < ident[:, None])
    pair_slot = jnp.sum(earlier.astype(jnp.int32), axis=1)
    slot_count = shards * CAP
    owners_mine = lax.dynamic_slice_in_dim(flat, here * per_shard, per_shard)
    pairs_mine = lax.dynamic_slice_in_dim(pair_slot, here * per_shard, per_shard)
    dest_flat = owners_mine * CAP + pairs_mine
    send_pick, send_valid = pick_index(dest_flat, slot_count)
    mine_owned = (flat == here).astype(jnp.int32)
    queue = jnp.arange(kept, dtype=jnp.int32)
    owned_match = mine_owned[None, :] * (ranks[None, :] == queue[:, None]).astype(jnp.int32)
    recv_flat = jnp.sum(owned_match * (source * CAP + pair_slot)[None, :], axis=1)
    back_pick, back_valid = pick_index(recv_flat, slot_count)
    blocks = (
        grad.reshape(row_blocks, width, col_blocks, width)
        .transpose(0, 2, 1, 3)
        .reshape(per_shard, width, width)
    )
    outgoing = jnp.where(send_valid[:, None, None], blocks[send_pick], jnp.zeros((), jnp.bfloat16))
    incoming = lax.all_to_all(
        outgoing.reshape(shards, CAP, width, width),
        "shard",
        split_axis=0,
        concat_axis=0,
        tiled=True,
    )
    owned = incoming.reshape(slot_count, width, width)[recv_flat]
    rotate_full = lax.all_gather(right_basis, "rep", axis=1, tiled=True)
    half = jnp.einsum("kab,kbc->kac", left_basis, owned, preferred_element_type=jnp.float32).astype(
        jnp.bfloat16
    )
    turned = jnp.einsum("kac,kcd->kad", half, rotate_full, preferred_element_type=jnp.float32)
    first = BETA_ONE * avg.astype(jnp.float32) + (1.0 - BETA_ONE) * turned
    second = BETA_TWO * avg_sq + (1.0 - BETA_TWO) * turned * turned
    scaled = (first / (jnp.sqrt(second) + EPSILON)).astype(jnp.bfloat16)
    back = jnp.einsum(
        "kad,ked->kae", scaled, rotate_full, preferred_element_type=jnp.float32
    ).astype(jnp.bfloat16)
    own_rows = lax.dynamic_slice_in_dim(owned, there * slice_rows, slice_rows, 1)
    own_cols = lax.dynamic_slice_in_dim(owned, there * slice_rows, slice_rows, 2)
    new_left_gram = BETA_TWO * left_gram + (1.0 - BETA_TWO) * jnp.einsum(
        "kab,kcb->kac", own_rows, owned, preferred_element_type=jnp.float32
    )
    new_right_gram = BETA_TWO * right_gram + (1.0 - BETA_TWO) * jnp.einsum(
        "kba,kbc->kac", own_cols, owned, preferred_element_type=jnp.float32
    )
    summed = jnp.einsum(
        "kab,kac->kbc",
        lax.all_gather(left_basis, "rep", axis=1, tiled=True),
        lax.all_gather(back, "rep", axis=1, tiled=True),
        preferred_element_type=jnp.float32,
    )
    finished = summed.astype(jnp.bfloat16)
    outgoing = jnp.where(
        back_valid[:, None, None], finished[back_pick], jnp.zeros((), jnp.bfloat16)
    )
    returned = lax.all_to_all(
        outgoing.reshape(shards, CAP, width, width),
        "shard",
        split_axis=0,
        concat_axis=0,
        tiled=True,
    )
    home = returned.reshape(slot_count, width, width)[dest_flat]
    update = (
        home.reshape(row_blocks, col_blocks, width, width).transpose(0, 2, 1, 3).reshape(grad.shape)
    )
    return (update, first.astype(jnp.bfloat16), second, new_left_gram, new_right_gram)


def solution(mesh):
    return jax.shard_map(
        body,
        mesh=mesh,
        in_specs=(
            P("shard", None),
            P(),
            P("shard", "rep", None),
            P("shard", "rep", None),
            P("shard", "rep", None),
            P("shard", "rep", None),
            P("shard", "rep", None),
            P("shard", "rep", None),
        ),
        out_specs=(
            P("shard", None),
            P("shard", "rep", None),
            P("shard", "rep", None),
            P("shard", "rep", None),
            P("shard", "rep", None),
        ),
        check_vma=False,
    )
```

profile of v0, /device:TPU:6, one launch (start us, length us, event | category | flops | bytes accessed | tf_op | source)
XLA Modules:
  0.0 405.6 jit_solution(8114019808177295108)
XLA Ops:
  7.2 0.8 copy.29
  7.9 0.1 eq.87
  8.0 0.2 convert_reduce_fusion
  8.2 0.1 compare_select_fusion
  8.3 0.1 convert_reduce_fusion.1
  8.4 2.3 copy.40
  10.7 0.1 bitcast_bitcast_fusion
  10.8 0.5 copy.32
  11.3 2.7 gather_fusion
  14.0 6.4 %copy.33 = bf16[16,2,256,256]{2,3,1,0:T(8,128)(2,1)} copy(bf16[16,2,256,256]{3,2,1,0:T(8,128)(2,1)} %bitcast.61) | data formatting | bytes 8388608 | tf_op jit(solution)/shard_map/gather | solution.py:57
  20.4 0.1 gt.23
  20.5 4.5 %broadcast_select_fusion = bf16[16,2,256,256]{2,3,1,0:T(8,128)(2,1)} fusion(bf16[16,2,256,256]{2,3,1,0:T(8,128)(2,1)} %copy.33, pred[16,2]{1,0:T(8,128)(4,1)S(1)} %gt.23), kind=kLoop, calls=%fused_computation.4 | loop fusion | flops 2097152 | bytes 8388640 | tf_op jit(solution)/shard_map/jit(_where)/select_n | solution.py:57
  25.0 10.1 %all-to-all-start = ((bf16[16,2,256,256]{2,3,1,0:T(8,128)(2,1)}), bf16[16,2,256,256]{2,3,1,0:T(8,128)(2,1)}, u32[]{:S(2)}, u32[]{:S(2)}) async-start(bf16[16,2,256,256]{2,3,1,0:T(8,128)(2,1)} %broadcast_select_fusion), calls=%async_computation | async-start | bytes 8388608 | tf_op jit(solution)/shard_map/all_to_all | solution.py:58
  35.2 0.0 all-gather.4.cloned.1.call-start
  35.2 0.7 all-gather.4.cloned.1.call-update
  35.9 0.0 all-gather.8.cloned.1.call-start
  36.0 0.7 all-gather.8.cloned.1.call-update
  36.7 0.0 all-gather.6.cloned.1.call-start
  36.7 0.1 eq.91
  36.8 0.6 reduce-window.6
  37.4 0.2 slice_reduce_fusion
  37.6 0.1 fusion.13
  37.8 0.1 multiply_reduce_fusion
  37.9 65.1 %all-to-all-done = bf16[16,2,256,256]{2,3,1,0:T(8,128)(2,1)} async-done(((bf16[16,2,256,256]{2,3,1,0:T(8,128)(2,1)}), bf16[16,2,256,256]{2,3,1,0:T(8,128)(2,1)}, u32[]{:S(2)}, u32[]{:S(2)}) %all-to-all-start) | async-done | bytes 4194336 | tf_op jit(solution)/shard_map/all_to_all | solution.py:58
  102.9 6.4 %copy.34 = bf16[16,2,256,256]{3,2,1,0:T(8,128)(2,1)} copy(bf16[16,2,256,256]{2,3,1,0:T(8,128)(2,1)} %all-to-all-done) | data formatting | bytes 8388608 | tf_op jit(solution)/shard_map/all_to_all | solution.py:58
  109.3 2.9 gather_fusion.1
  112.3 16.9 %all-gather.4.cloned.1.call-done = bf16[16,256,256]{2,1,0:T(8,128)(2,1)} async-done(((bf16[16,8,256]{2,1,0:T(8,128)(2,1)}), bf16[16,256,256]{2,1,0:T(8,128)(2,1)}) %all-gather.4.cloned.1.call-update) | async-done | bytes 2097168 | tf_op jit(solution)/shard_map/all_gather | solution.py:66
  129.2 0.0 copy-done.1
  129.2 0.0 copy-done.2
  129.2 0.0 copy-done.3
  129.2 2.9 fusion.6
  132.1 2.9 convolution_convert_fusion
  135.0 0.0 all-gather.6.cloned.1.call-update
  135.0 0.1 convert_reduce_fusion.2
  135.1 0.1 gt.21
  135.3 83.9 %all-gather.8.cloned.1.call-done = bf16[16,256,256]{2,1,0:T(8,128)(2,1)} async-done(((bf16[16,8,256]{2,1,0:T(8,128)(2,1)}), bf16[16,256,256]{2,1,0:T(8,128)(2,1)}) %all-gather.8.cloned.1.call-update) | async-done | bytes 2097168 | tf_op jit(solution)/shard_map/all_gather | solution.py:87
  219.2 87.8 %all-gather.6.cloned.1.call-done = bf16[16,256,256]{2,1,0:T(8,128)(2,1)} async-done(((bf16[16,8,256]{2,1,0:T(8,128)(2,1)}), bf16[16,256,256]{2,1,0:T(8,128)(2,1)}) %all-gather.6.cloned.1.call-update) | async-done | bytes 2097168 | tf_op jit(solution)/shard_map/all_gather | solution.py:88
  307.0 4.3 %convert_bitcast_fusion = bf16[16,256,256]{1,2,0:T(8,128)(2,1)} fusion(bf16[16,256,256]{2,1,0:T(8,128)(2,1)} %all-gather.6.cloned.1.call-done, bf16[16,256,256]{2,1,0:T(8,128)(2,1)} %all-gather.8.cloned.1.call-done), kind=kOutput, calls=%fused_computation.7 | convolution fusion | flops 537919488 | bytes 6291456 | tf_op jit(solution)/shard_map/kab,kac->kbc/dot_general | solution.py:85
  311.3 4.3 %gather_fusion.2 = bf16[32,256,256]{1,2,0:T(8,128)(2,1)} fusion(bf16[16,256,256]{1,2,0:T(8,128)(2,1)} %convert_bitcast_fusion, s32[1024]{0:T(1024)S(1)} %pad_clamp_fusion.1), kind=kCustom, calls=%fused_computation.2 | custom fusion | bytes 8388736 | tf_op jit(solution)/shard_map/gather | solution.py:93
  315.7 4.5 %broadcast_select_fusion.1 = bf16[16,2,256,256]{2,3,1,0:T(8,128)(2,1)} fusion(bf16[16,2,256,256]{2,3,1,0:T(8,128)(2,1)} %bitcast.60, pred[16,2]{1,0:T(8,128)(4,1)S(1)} %gt.21), kind=kLoop, calls=%fused_computation.5 | loop fusion | flops 2097152 | bytes 8388640 | tf_op jit(solution)/shard_map/jit(_where)/select_n | solution.py:92
  320.2 5.0 %all-to-all-start.1 = ((bf16[16,2,256,256]{2,3,1,0:T(8,128)(2,1)}), bf16[16,2,256,256]{2,3,1,0:T(8,128)(2,1)}, u32[]{:S(2)}, u32[]{:S(2)}) async-start(bf16[16,2,256,256]{2,3,1,0:T(8,128)(2,1)} %broadcast_select_fusion.1), calls=%async_computation.1 | async-start | bytes 8388608 | tf_op jit(solution)/shard_map/all_to_all | solution.py:95
  325.2 1.6 fusion
  326.8 1.3 fusion.1
  328.1 58.5 %all-to-all-done.1 = bf16[16,2,256,256]{2,3,1,0:T(8,128)(2,1)} async-done(((bf16[16,2,256,256]{2,3,1,0:T(8,128)(2,1)}), bf16[16,2,256,256]{2,3,1,0:T(8,128)(2,1)}, u32[]{:S(2)}, u32[]{:S(2)}) %all-to-all-start.1) | async-done | bytes 4194336 | tf_op jit(solution)/shard_map/all_to_all | solution.py:95
  386.6 6.4 %copy.35 = bf16[16,2,256,256]{3,2,1,0:T(8,128)(2,1)} copy(bf16[16,2,256,256]{2,3,1,0:T(8,128)(2,1)} %all-to-all-done.1) | data formatting | bytes 8388608 | tf_op jit(solution)/shard_map/all_to_all | solution.py:95
  393.0 2.9 gather_fusion.3
  395.9 1.2 copy.36
  397.1 2.0 copy.41
  (24 shorter events, 0.1 us)
Async XLA Ops:
  25.0 77.9 %all-to-all-start = ((bf16[16,2,256,256]{2,3,1,0:T(8,128)(2,1)}), bf16[16,2,256,256]{2,3,1,0:T(8,128)(2,1)}, u32[]{:S(2)}, u32[]{:S(2)}) async-start(bf16[16,2,256,256]{2,3,1,0:T(8,128)(2,1)} %broadcast_select_fusion), calls=%async_computation | async-start | bytes 8388608 | tf_op jit(solution)/shard_map/all_to_all | solution.py:58
  35.2 94.0 %all-gather.4.cloned.1.call-start = ((), (), s32[]{:S(2)}) async-start(), calls=%async_computation.2 | async-start | bytes 2162688 | tf_op jit(solution)/shard_map/all_gather | solution.py:66
  35.9 183.3 %all-gather.8.cloned.1.call-start = ((), (), s32[]{:S(2)}) async-start(), calls=%async_computation.4 | async-start | bytes 2162688 | tf_op jit(solution)/shard_map/all_gather | solution.py:87
  36.7 270.4 %all-gather.6.cloned.1.call-start = ((), (), s32[]{:S(2)}) async-start(), calls=%async_computation.3 | async-start | bytes 2162688 | tf_op jit(solution)/shard_map/all_gather | solution.py:88
  109.3 19.9 %copy-start.1 = (bf16[16,8,256]{2,1,0:T(8,128)(2,1)S(1)}, bf16[16,8,256]{2,1,0:T(8,128)(2,1)}, u32[]{:S(2)}) copy-start(bf16[16,8,256]{2,1,0:T(8,128)(2,1)} %param.12) | copy-start | bytes 196612
  109.3 19.9 %copy-start.2 = (bf16[16,8,256]{2,1,0:T(8,128)(2,1)S(1)}, bf16[16,8,256]{2,1,0:T(8,128)(2,1)}, u32[]{:S(2)}) copy-start(bf16[16,8,256]{2,1,0:T(8,128)(2,1)} %param.10) | copy-start | bytes 196612
  109.3 19.9 %copy-start.3 = (f32[16,8,256]{2,1,0:T(8,128)S(1)}, f32[16,8,256]{2,1,0:T(8,128)}, u32[]{:S(2)}) copy-start(f32[16,8,256]{2,1,0:T(8,128)} %param.13) | copy-start | bytes 393220
  132.1 179.3 %copy-start = (f32[16,8,256]{2,1,0:T(8,128)}, f32[16,8,256]{2,1,0:T(8,128)S(1)}, u32[]{:S(2)}) copy-start(f32[16,8,256]{2,1,0:T(8,128)S(1)} %get-tuple-element.12) | copy-start | bytes 393220
  320.2 5.0 %copy-start.4 = (f32[16,8,256]{2,1,0:T(8,128)S(1)}, f32[16,8,256]{2,1,0:T(8,128)}, u32[]{:S(2)}) copy-start(f32[16,8,256]{2,1,0:T(8,128)} %param.15) | copy-start | bytes 393220
  320.2 66.4 %all-to-all-start.1 = ((bf16[16,2,256,256]{2,3,1,0:T(8,128)(2,1)}), bf16[16,2,256,256]{2,3,1,0:T(8,128)(2,1)}, u32[]{:S(2)}, u32[]{:S(2)}) async-start(bf16[16,2,256,256]{2,3,1,0:T(8,128)(2,1)} %broadcast_select_fusion.1), calls=%async_computation.1 | async-start | bytes 8388608 | tf_op jit(solution)/shard_map/all_to_all | solution.py:95
  325.1 1.7 copy-start.5
Sparse Core Ops, SparseCore 0:
  39.1 90.0 all-gather.3
  132.3 86.8 all-gather.7
  222.8 84.1 all-gather.5
where the time goes:
time: 407 us; the launch traced here: 406 us
  waiting for transfers between devices  314 us (77%)
  local copies, waits for them, and re-layouts  39.4 us (10%)
  starting transfers between devices  15.2 us (4%)
  between operations  13.9 us (3%)
  matrix products  13.1 us (3%)
  other arithmetic  10.4 us (3%)
    all_to_all x2, waiting for transfers between devices, body(): lax.all_to_all(outgoing.reshape(shards, CAP, width, width), 'shard', spli...  124 us
    all_gather x1, waiting for transfers between devices, body(): lax.all_gather(back, 'rep', axis=1, tiled=True)  87.8 us
    all_gather x1, waiting for transfers between devices, body(): lax.all_gather(left_basis, 'rep', axis=1, tiled=True)  83.9 us
    all_gather x1, waiting for transfers between devices, body(): rotate_full = lax.all_gather(right_basis, 'rep', axis=1, tiled=True)  16.9 us
    all_to_all x2, starting transfers between devices, body(): lax.all_to_all(outgoing.reshape(shards, CAP, width, width), 'shard', spli...  15.1 us
    all_to_all x2, local copies, waits for them, and re-layouts, body(): lax.all_to_all(outgoing.reshape(shards, CAP, width, width), 'shard', spli...  12.8 us
    gather x2, local copies, waits for them, and re-layouts, body(): blocks[send_pick]  9.14 us
  transfers between devices with their start and end apart: 5, of which 5 were waited for; matrix products, arithmetic and copies ran while one was open for 5% of the time, Pallas kernels for 0%

commit v1 on v0

v1 whole, which is shorter than its diff:
```python
import functools

import jax
import jax.numpy as jnp
from jax import lax
from jax.experimental import pallas as pl
from jax.experimental.pallas import tpu as pltpu
from jax.sharding import PartitionSpec as P

CAP = 2
BETA_ONE = 0.9
BETA_TWO = 0.95
EPSILON = 1e-08

YS = 8
ZS = 4
REPS = YS * ZS
SHARDS = 16
KEPT = 16
W = 256
PR, PC = 16, 128
PARTS = 2
FAR_Y = (4, 3, 5, 2, 6, 1, 7, 0)
FAR_Z = (2, 1, 3, 0)
MESH = pl.DeviceIdType.MESH


def routing(owner, here):
    flat = owner.T.reshape(-1)
    place = jnp.arange(flat.shape[0], dtype=jnp.int32)
    ident = place % owner.shape[0] * owner.shape[1] + place // owner.shape[0]
    source = ident // KEPT
    same = (flat[:, None] == flat[None, :]) & (ident[None, :] < ident[:, None])
    rank = jnp.sum(same.astype(jnp.int32), axis=1)
    pair = jnp.sum((same & (source[:, None] == source[None, :])).astype(jnp.int32), axis=1)
    local = jnp.arange(KEPT, dtype=jnp.int32)
    slots = jnp.arange(SHARDS * CAP, dtype=jnp.int32)
    mine = (ident[None, :] == here * KEPT + local[:, None]).astype(jnp.int32)
    dest = jnp.sum(mine * (flat * CAP + pair)[None, :], axis=1)
    owned = ((flat == here)[None, :] & (rank[None, :] == local[:, None])).astype(jnp.int32)
    recv = jnp.sum(owned * (source * CAP + pair)[None, :], axis=1)
    send_pick = jnp.sum((dest[None, :] == slots[:, None]).astype(jnp.int32) * local[None, :], axis=1)
    back_pick = jnp.sum((recv[None, :] == slots[:, None]).astype(jnp.int32) * local[None, :], axis=1)
    return jnp.concatenate([send_pick, recv, back_pick, dest])


def fold(x):
    x = x.astype(jnp.float32)
    return jnp.concatenate([x[:, :, :PC], x[:, :, PC:]], axis=1).astype(jnp.bfloat16)


def unfold(x):
    x = x.astype(jnp.float32)
    return jnp.concatenate([x[:, :8, :], x[:, 8:, :]], axis=2)


def nn(a, b):
    return lax.dot_general(a, b, (((1,), (0,)), ((), ())), preferred_element_type=jnp.float32)


def nt(a, b):
    return lax.dot_general(a, b, (((1,), (1,)), ((), ())), preferred_element_type=jnp.float32)


def tn(a, b):
    return lax.dot_general(a, b, (((0,), (0,)), ((), ())), preferred_element_type=jnp.float32)


def wait_bytes(ref, sem):
    pltpu.make_async_copy(ref, ref, sem).wait()


def kernel(
    idx, left_h, right_h, avg_h, avg_sq_h, grad, left_gram_h, right_gram_h,
    update, new_avg, new_avg_sq, new_left, new_right,
    left, right, avg, avg_sq, whole, left_gram, right_gram,
    folded, bases_out, moments_out, bases_in, moments_in, bases_row, moments_row, bases, moments,
    rsend, rbuf, grams, tsend, trecv,
    load_sem, send_sem, recv_sem, z_send, ag_send, ag_recv,
):
    r = lax.axis_index("rep")
    s = lax.axis_index("shard")
    y, z = r // ZS, r % ZS
    z_half, z_odd = z // 2, z % 2
    p0 = (y + s) % 2
    is_hub = z_odd == p0

    def wrap(v, n):
        return jnp.where(v >= n, v - n, v)

    ys = [wrap(y + t, YS) for t in range(YS)]
    zs = [wrap(z + t, ZS) for t in range(ZS)]
    z_low, x, core = s // 8, s % 8 // 2, s % 2
    xs = [wrap(x + t, 4) for t in range(4)]
    ss = [
        (1 - z_low if a else z_low) * 8 + xs[b] * 2 + (1 - core if c else core)
        for a, b, c in (
            (1, 2, 1), (1, 2, 0), (0, 2, 1), (0, 2, 0), (1, 1, 1), (1, 1, 0), (1, 3, 1), (1, 3, 0),
            (0, 1, 1), (0, 1, 0), (0, 3, 1), (0, 3, 0), (1, 0, 1), (1, 0, 0), (0, 0, 1),
        )
    ]

    def to(rep):
        return dict(device_id={"rep": rep}, device_id_type=MESH)

    def over(shard):
        return dict(device_id={"shard": shard}, device_id_type=MESH)

    loads = [
        pltpu.make_async_copy(src, dst, load_sem.at[n])
        for n, (src, dst) in enumerate(
            [(left_h, left), (right_h, right), (avg_h, avg), (avg_sq_h, avg_sq),
             (grad, whole), (left_gram_h, left_gram), (right_gram_h, right_gram)]
        )
    ]
    for copy in loads[:4]:
        copy.start()

    barrier = pltpu.get_barrier_semaphore()
    for peer in ss:
        pl.semaphore_signal(barrier, inc=1, **over(peer))

    @pl.when(is_hub)
    def _():
        for t in FAR_Y[:-1]:
            for v in FAR_Z[:-1]:
                pl.semaphore_signal(barrier, inc=1, **to(ys[t] * ZS + zs[v]))

    for t in FAR_Y[:-1]:
        pl.semaphore_signal(barrier, inc=1, **to(ys[t] * ZS + z))
    for v in FAR_Z[:-1]:
        pl.semaphore_signal(barrier, inc=1, **to(y * ZS + zs[v]))

    for n, ref in enumerate((left, right, avg, avg_sq)):
        loads[n].wait()
        folded[:, n] = fold(ref[...])
    for n in range(SHARDS * CAP):
        block = folded[idx[SHARDS * CAP + KEPT + n]]
        bases_out[n] = block[:2]
        moments_out[n] = block[2:]
    pl.semaphore_wait(barrier, jnp.where(is_hub, SHARDS - 1 + 21, SHARDS - 1 + 20))

    mine = pl.ds(s * CAP, CAP)

    def exchange(src, dst, n):
        pltpu.make_async_copy(src.at[mine], dst.at[mine], recv_sem.at[n]).start()
        for peer in ss:
            pltpu.make_async_remote_copy(
                src.at[pl.ds(peer * CAP, CAP)], dst.at[mine], send_sem.at[n], recv_sem.at[n], **over(peer)
            ).start()

    exchange(bases_out, bases_in, 0)
    exchange(moments_out, moments_in, 1)
    for copy in loads[4:]:
        copy.start()

    def to_hub(src, dst, n):
        for t in FAR_Y:
            p = p0 if t % 2 == 0 else 1 - p0
            for b in (1 - z_half, z_half):
                block, h = 2 * ys[t] + b, ys[t] * ZS + 2 * b + p

                def remote(block=block, h=h):
                    pltpu.make_async_remote_copy(
                        src.at[block], dst.at[r], send_sem.at[n], recv_sem.at[n], **to(h)
                    ).start()

                if t == 0:
                    pl.when(h != r)(remote)

                    @pl.when(h == r)
                    def _(block=block):
                        pltpu.make_async_copy(src.at[block], dst.at[r], recv_sem.at[n]).start()
                else:
                    remote()

    for n, (got, row, out) in enumerate(
        ((bases_in, bases_row, bases), (moments_in, moments_row, moments))
    ):
        wait_bytes(got, recv_sem.at[n])
        for b in range(KEPT):
            row[b] = got[idx[2 * SHARDS * CAP + KEPT + b]]
        to_hub(row, out, 2 + n)

    block_me = 2 * y + z_half
    row_of = [pl.multiple_of(ys[t] // 4 * W, W) for t in range(YS)]
    col_of = [pl.multiple_of(ys[t] % 4 * (2 * W), W) for t in range(YS)]

    @pl.when(is_hub)
    def _():
        loads[4].wait()
        here = (pl.ds(row_of[0], W), pl.ds(pl.multiple_of(col_of[0] + z_half * W, W), W))
        g = whole[here]
        wait_bytes(bases, recv_sem.at[2])
        lb = unfold(bases[:, 0]).reshape(W, W).astype(jnp.bfloat16)
        rb = unfold(bases[:, 1]).reshape(W, W).astype(jnp.bfloat16)
        half = nn(lb, g).astype(jnp.bfloat16)
        turned = nn(half, rb)
        wait_bytes(moments, recv_sem.at[3])
        m0 = unfold(moments[:, 0]).reshape(W, W)
        v0 = unfold(moments[:, 1]).reshape(W, W)
        first = BETA_ONE * m0 + (1.0 - BETA_ONE) * turned
        second = BETA_TWO * v0 + (1.0 - BETA_TWO) * turned * turned
        scaled = (first / (jnp.sqrt(second) + EPSILON)).astype(jnp.bfloat16)
        back = nt(scaled, rb).astype(jnp.bfloat16)
        update[here] = tn(lb, back).astype(jnp.bfloat16)
        rsend[...] = fold(turned.reshape(REPS, 8, W))

    ups = (ys[1] * ZS + z, ys[7] * ZS + z)
    z_pair = 2 * z_half + 1 - z_odd
    z_next = jnp.where(z_odd == 1, zs[1], zs[3])
    pending = []
    names = {}

    def region(t, bit, rows):
        return update.at[
            pl.ds(pl.multiple_of(row_of[t] + rows[0], 16), rows[1] - rows[0]),
            pl.ds(pl.multiple_of(col_of[t] + bit * W, W), W),
        ]

    def push(ref, peer, key):
        n = names.setdefault(key, len(names))
        copy = pltpu.make_async_remote_copy(ref, ref, ag_send.at[n], ag_recv.at[n], **to(peer))
        copy.start()
        return copy

    def pull(ref, key):
        wait_bytes(ref, ag_recv.at[names[key]])

    bits = (z_half, 1 - z_half)
    parts = [(n * W // PARTS, (n + 1) * W // PARTS) for n in range(PARTS)]

    @pl.when(is_hub)
    def _():
        for m, rows in enumerate(parts):
            ref = region(0, bits[0], rows)
            for n, (c, peer) in enumerate(((1, zs[2]), (1, z_next), (0, z_pair))):
                key = names.setdefault(("z", c, m), len(names))
                pltpu.make_async_remote_copy(
                    ref, ref, z_send.at[3 * m + n], ag_recv.at[key], **to(y * ZS + peer)
                ).start()

    def y_rows(m, d, way):
        lo, hi = parts[m]
        if d < YS // 2:
            return lo, hi
        mid = (lo + hi) // 2
        return (lo, mid) if way == 0 else (mid, hi)

    def far(d, way):
        return (-d if way == 0 else d) % YS

    def y_push(c, m, d, way):
        ref = region(far(d - 1, way), bits[c], y_rows(m, d, way))
        pending.append(push(ref, ups[way], ("y", c, m, d, way)))

    def z_step(c, m):
        ref = region(0, bits[c], parts[m])
        if c == 0:
            pl.when(jnp.logical_not(is_hub))(lambda: pull(ref, ("z", c, m)))
        else:
            pull(ref, ("z", c, m))
        for way in range(2):
            y_push(c, m, 1, way)

    def y_step(c, m, d):
        for way in range(2):
            pull(region(far(d, way), bits[c], y_rows(m, d, way)), ("y", c, m, d, way))
            if d < YS // 2:
                y_push(c, m, d + 1, way)

    strip_at = pl.multiple_of(PR * (2 * y + z_half), PR)
    picks = (
        lax.broadcasted_iota(jnp.int32, (PR, W), 1)
        == lax.broadcasted_iota(jnp.int32, (PR, W), 0) + strip_at
    ).astype(jnp.float32).astype(jnp.bfloat16)

    def gram_rows(blocks):
        for b in blocks:
            i, j = b // 8, b % 8
            g = whole[i * W : (i + 1) * W, j * W : (j + 1) * W]
            strip = whole[pl.ds(i * W + strip_at, PR), j * W : (j + 1) * W]
            both = nt(jnp.concatenate([strip, picks], axis=0), g)
            wide = nn(both[PR:].astype(jnp.bfloat16), g)
            for n, v in enumerate((both[:PR], wide)):
                v = jnp.where(z_odd == 1, v[8:], v[:8])
                grams[b, n] = jnp.concatenate([v[:, :PC], v[:, PC:]], axis=0).astype(jnp.bfloat16)

    def side(n):
        if n == 0:

            @pl.when(jnp.logical_not(is_hub))
            def _():
                loads[4].wait()

        if n < YS // 2:

            @pl.when(is_hub)
            def _():
                for t in FAR_Y[2 * n : 2 * n + 2]:
                    for v in FAR_Z:
                        q = ys[t] * ZS + zs[v]
                        if t or v:
                            pltpu.make_async_remote_copy(
                                rsend.at[q], rbuf.at[block_me], send_sem.at[4], recv_sem.at[4], **to(q)
                            ).start()
                        else:
                            pltpu.make_async_copy(rsend.at[r], rbuf.at[block_me], recv_sem.at[4]).start()

        if n < KEPT // 2:
            gram_rows((2 * n, 2 * n + 1))
        elif n == KEPT // 2:
            wait_bytes(rbuf, recv_sem.at[4])
            for m in range(SHARDS * CAP):
                b = idx[m]
                tsend[m, 0] = rbuf[b]
                tsend[m, 1:] = grams[b]
            exchange(tsend, trecv, 5)

    def own_rows():
        wait_bytes(trecv, recv_sem.at[5])
        for copy in loads[5:]:
            copy.wait()
        for n in range(KEPT):
            turned, gl, gr = unfold(trecv[idx[SHARDS * CAP + n]])
            new_avg[n] = (BETA_ONE * avg[n].astype(jnp.float32) + (1.0 - BETA_ONE) * turned).astype(jnp.bfloat16)
            new_avg_sq[n] = BETA_TWO * avg_sq[n] + (1.0 - BETA_TWO) * turned * turned
            new_left[n] = BETA_TWO * left_gram[n] + (1.0 - BETA_TWO) * gl
            new_right[n] = BETA_TWO * right_gram[n] + (1.0 - BETA_TWO) * gr

    order = [(z_step, 0, m) for m in range(PARTS)]
    for m in range(PARTS):
        order += [(z_step, 1, m), (y_step, 0, m, 1)]
    order += [(y_step, 1, m, 1) for m in range(PARTS)]
    for d in (2, 3, 4):
        order += [(y_step, c, m, d) for c in range(2) for m in range(PARTS)]
    count = 0
    for step, *args in order[:-2]:
        step(*args)
        if count <= KEPT // 2:
            side(count)
        count += 1
        if count == len(order) - 4:
            own_rows()

    for copy in pending:
        copy.wait_send()
    for n, ref in ((0, bases_out), (1, moments_out), (5, tsend)):
        wait_bytes(ref.at[pl.ds(0, CAP * (SHARDS - 1))], send_sem.at[n])

    @pl.when(is_hub)
    def _():
        wait_bytes(bases_row.at[pl.ds(0, KEPT - 1)], send_sem.at[2])
        wait_bytes(moments_row.at[pl.ds(0, KEPT - 1)], send_sem.at[3])
        wait_bytes(rsend.at[pl.ds(0, REPS - 1)], send_sem.at[4])
        for n in range(3 * PARTS):
            wait_bytes(region(0, bits[0], parts[n // 3]), z_send.at[n])

    @pl.when(jnp.logical_not(is_hub))
    def _():
        wait_bytes(bases_row, send_sem.at[2])
        wait_bytes(moments_row, send_sem.at[3])

    for step, *args in order[-2:]:
        step(*args)


def store_kernel(*refs):
    count = len(refs) // 2
    sems = refs[-1]
    copies = []
    for n in range(count):
        src, dst = refs[n], refs[count + n]
        parts = 8 if n == 0 else 1
        size = src.shape[0] // parts
        for p in range(parts):
            rows = pl.ds(p * size, size)
            copies.append(pltpu.make_async_copy(src.at[rows], dst.at[rows], sems.at[len(copies)]))
    for copy in copies:
        copy.start()
    for copy in copies:
        copy.wait()


def body(grad, owner, left_basis, right_basis, avg, avg_sq, left_gram, right_gram):
    here = lax.axis_index("shard")
    idx = routing(owner, here)
    vmem = pl.BlockSpec(memory_space=pltpu.VMEM)
    hbm = pl.BlockSpec(memory_space=pltpu.HBM)
    bf16, f32 = jnp.bfloat16, jnp.float32
    slots = SHARDS * CAP
    rows = (KEPT, 8, W)
    outs = [jax.ShapeDtypeStruct(x.shape, x.dtype) for x in (grad, avg, avg_sq, left_gram, right_gram)]
    operands = [
        pltpu.with_memory_space_constraint(x, pltpu.HBM)
        for x in (left_basis, right_basis, avg, avg_sq, grad, left_gram, right_gram)
    ]
    results = pl.pallas_call(
        kernel,
        out_shape=outs,
        in_specs=[pl.BlockSpec(memory_space=pltpu.SMEM)] + [hbm] * 7,
        out_specs=[vmem] * 5,
        scratch_shapes=[
            pltpu.VMEM(rows, bf16),
            pltpu.VMEM(rows, bf16),
            pltpu.VMEM(rows, bf16),
            pltpu.VMEM(rows, f32),
            pltpu.VMEM(grad.shape, bf16),
            pltpu.VMEM(rows, f32),
            pltpu.VMEM(rows, f32),
            pltpu.VMEM((KEPT, 4, PR, PC), bf16),
            pltpu.VMEM((slots, 2, PR, PC), bf16),
            pltpu.VMEM((slots, 2, PR, PC), bf16),
            pltpu.VMEM((slots, 2, PR, PC), bf16),
            pltpu.VMEM((slots, 2, PR, PC), bf16),
            pltpu.VMEM((KEPT, 2, PR, PC), bf16),
            pltpu.VMEM((KEPT, 2, PR, PC), bf16),
            pltpu.VMEM((REPS, 2, PR, PC), bf16),
            pltpu.VMEM((REPS, 2, PR, PC), bf16),
            pltpu.VMEM((REPS, PR, PC), bf16),
            pltpu.VMEM((KEPT, PR, PC), bf16),
            pltpu.VMEM((KEPT, 2, PR, PC), bf16),
            pltpu.VMEM((slots, 3, PR, PC), bf16),
            pltpu.VMEM((slots, 3, PR, PC), bf16),
            pltpu.SemaphoreType.DMA((7,)),
            pltpu.SemaphoreType.DMA((6,)),
            pltpu.SemaphoreType.DMA((6,)),
            pltpu.SemaphoreType.DMA((3 * PARTS,)),
            pltpu.SemaphoreType.DMA((18 * PARTS,)),
            pltpu.SemaphoreType.DMA((18 * PARTS,)),
        ],
        compiler_params=pltpu.CompilerParams(
            collective_id=0, has_side_effects=True, vmem_limit_bytes=40 * 1024 * 1024
        ),
        cost_estimate=pl.CostEstimate(flops=12 * W**3, bytes_accessed=6 << 20, transcendentals=0),
        name="soap_step",
    )(idx, *operands)
    return tuple(
        pl.pallas_call(
            store_kernel,
            out_shape=outs,
            in_specs=[pl.BlockSpec(memory_space=pl.ANY)] * 5,
            out_specs=[hbm] * 5,
            scratch_shapes=[pltpu.SemaphoreType.DMA((12,))],
            compiler_params=pltpu.CompilerParams(vmem_limit_bytes=4 * 1024 * 1024),
            cost_estimate=pl.CostEstimate(flops=0, bytes_accessed=5 << 20, transcendentals=0),
            name="store",
        )(*results)
    )


def solution(mesh):
    rows = P("shard", "rep", None)
    return jax.shard_map(
        body,
        mesh=mesh,
        in_specs=(P("shard", None), P(), rows, rows, rows, rows, rows, rows),
        out_specs=(P("shard", None), rows, rows, rows, rows),
        check_vma=False,
    )
```

time: 407 us -> 65.7 us (0.16)
  waiting for transfers between devices: 314 us -> 0 us
  Pallas kernels: 0 us -> 63.2 us
  local copies, waits for them, and re-layouts: 39.4 us -> 0.77 us
  starting transfers between devices: 15.2 us -> 0 us
  between operations: 13.9 us -> 0.66 us
  matrix products: 13.1 us -> 0 us
  other arithmetic: 10.4 us -> 0.88 us
    all_gather x3 -> x0, waiting for transfers between devices: 189 us -> none  [the longest x1 87.8 us: body(): lax.all_gather(back, 'rep', axis=1, tiled=True)]
    all_to_all x2 -> x0, waiting for transfers between devices: 124 us -> none  [body(): lax.all_to_all(outgoing.reshape(shards, CAP, width, width), 'shard', spli...]
    pallas_call x0 -> x2, Pallas kernels: none -> 63.2 us  [the longest x1 61.6 us: body(): pl.pallas_call(kernel, out_shape=outs, in_specs=[pl.BlockSpec(memory_spac...]
    gather x5 -> x0, local copies, waits for them, and re-layouts: 19.2 us -> none  [the longest x2 9.14 us: body(): blocks[send_pick]]
    all_to_all x2 -> x0, starting transfers between devices: 15.1 us -> none  [body(): lax.all_to_all(outgoing.reshape(shards, CAP, width, width), 'shard', spli...]
    dot_general x5 -> x0, matrix products: 13.1 us -> none  [the longest x1 4.31 us: body(): jnp.einsum('kab,kac->kbc', lax.all_gather(left_basis, 'rep', axis=1, tile...]
    all_to_all x2 -> x0, local copies, waits for them, and re-layouts: 12.8 us -> none  [body(): lax.all_to_all(outgoing.reshape(shards, CAP, width, width), 'shard', spli...]
    select_n x6 -> x1, other arithmetic: 9.1 us -> 0.01 us  [routing(): source = ident // KEPT]
  transfers between devices with their start and end apart: 5 -> 0, of which waited for: 5 -> 0; matrix products, arithmetic and copies ran while one was open for 5% -> 0% of each run, Pallas kernels for 0% -> 0%
where the time goes in v1:
time: 65.7 us; the launch traced here: 65.5 us
  Pallas kernels  63.2 us (96%)
  other arithmetic  0.88 us (1%)
  local copies, waits for them, and re-layouts  0.77 us (1%)
  between operations  0.66 us (1%)
    pallas_call x1, Pallas kernels, body(): pl.pallas_call(kernel, out_shape=outs, in_specs=[pl.BlockSpec(memory_spac...  61.6 us
    pallas_call x1, Pallas kernels, body(): pl.pallas_call(store_kernel, out_shape=outs, in_specs=[pl.BlockSpec(memor...  1.56 us

profile of v1, /device:TPU:6, one launch (start us, length us, event | category | flops | bytes accessed | tf_op | source)
XLA Modules:
  0.0 65.5 jit_solution(7263844225404987572)
XLA Ops:
  0.6 0.8 %reshape.120 = s32[256]{0:T(256)S(1)} reshape(s32[8,32]{1,0:T(8,128)} %bitcast.1) | data formatting | bytes 2048 | tf_op jit(solution)/shard_map/reshape | solution.py:29
  1.4 0.3 convert_reduce_fusion
  1.7 0.2 select_reduce_fusion.1
  1.9 0.1 select_reduce_fusion
  2.0 0.1 select_reduce_fusion.2
  2.1 0.1 select_reduce_fusion.3
  2.2 0.1 pad_add_fusion.idx
  2.3 61.6 %soap_step.1 = (bf16[512,2048]{1,0:T(8,128)(2,1)S(1)}, bf16[16,8,256]{2,1,0:T(8,128)(2,1)S(1)}, f32[16,8,256]{2,1,0:T(8,128)S(1)}, f32[16,8,256]{2,1,0:T(8,128)S(1)}, f32[16,8,256]{2,1,0:T(8,128)S(1)}) custom-call(s32[96]{0:T(128)S(1)} %pad_add_fusion.idx, bf16[16,8,256]{2,1,0:T(8,128)(2,1)} %left_h.1, bf16[16,8,256]{2,1,0:T(8,128)(2,1)} %right_h.1, ...), custom_call_target="tpu_custom_call" | custom-call | flops 201326592 | bytes 6291456 | tf_op jit(solution)/shard_map/soap_step/pallas_call | solution.py:398
  63.9 1.6 %store.1 = (bf16[512,2048]{1,0:T(8,128)(2,1)}, bf16[16,8,256]{2,1,0:T(8,128)(2,1)}, f32[16,8,256]{2,1,0:T(8,128)}, f32[16,8,256]{2,1,0:T(8,128)}, f32[16,8,256]{2,1,0:T(8,128)}) custom-call(bf16[512,2048]{1,0:T(8,128)(2,1)S(1)} %get-tuple-element.10.refs_0_, bf16[16,8,256]{2,1,0:T(8,128)(2,1)S(1)} %get-tuple-element.11.refs_1_, ...), custom_call_target="tpu_custom_call" | custom-call | bytes 5242880 | tf_op jit(solution)/shard_map/store/pallas_call | solution.py:439
  (4 shorter events, 0.0 us)

commit v2 on v1

--- a/solution.py
+++ b/solution.py
@@ -19,7 +19,7 @@
 KEPT = 16
 W = 256
 PR, PC = 16, 128
-PARTS = 2
+PARTS = 4
 FAR_Y = (4, 3, 5, 2, 6, 1, 7, 0)
 FAR_Z = (2, 1, 3, 0)
 MESH = pl.DeviceIdType.MESH
@@ -122,14 +122,10 @@
 
     @pl.when(is_hub)
     def _():
-        for t in FAR_Y[:-1]:
-            for v in FAR_Z[:-1]:
-                pl.semaphore_signal(barrier, inc=1, **to(ys[t] * ZS + zs[v]))
-
-    for t in FAR_Y[:-1]:
-        pl.semaphore_signal(barrier, inc=1, **to(ys[t] * ZS + z))
-    for v in FAR_Z[:-1]:
-        pl.semaphore_signal(barrier, inc=1, **to(y * ZS + zs[v]))
+        for t in FAR_Y:
+            for v in FAR_Z:
+                if t or v:
+                    pl.semaphore_signal(barrier, inc=1, **to(ys[t] * ZS + zs[v]))
 
     for n, ref in enumerate((left, right, avg, avg_sq)):
         loads[n].wait()
@@ -138,7 +134,7 @@
         block = folded[idx[SHARDS * CAP + KEPT + n]]
         bases_out[n] = block[:2]
         moments_out[n] = block[2:]
-    pl.semaphore_wait(barrier, jnp.where(is_hub, SHARDS - 1 + 21, SHARDS - 1 + 20))
+    pl.semaphore_wait(barrier, jnp.where(is_hub, SHARDS - 1 + KEPT - 1, SHARDS - 1 + KEPT))
 
     mine = pl.ds(s * CAP, CAP)
 

time: 65.7 us -> 65.9 us (level)
  no operation moved by 1% of the time
where the time goes in v2:
time: 65.9 us; the launch traced here: 65.6 us
  Pallas kernels  63.3 us (96%)
  other arithmetic  0.88 us (1%)
  local copies, waits for them, and re-layouts  0.77 us (1%)
  between operations  0.66 us (1%)
    pallas_call x1, Pallas kernels, body(): pl.pallas_call(kernel, out_shape=outs, in_specs=[pl.BlockSpec(memory_spac...  61.7 us
    pallas_call x1, Pallas kernels, body(): pl.pallas_call(store_kernel, out_shape=outs, in_specs=[pl.BlockSpec(memor...  1.56 us

profile of v2, /device:TPU:6, one launch (start us, length us, event | category | flops | bytes accessed | tf_op | source)
XLA Modules:
  0.0 65.6 jit_solution(9117154267922786862)
XLA Ops:
  0.6 0.8 %reshape.120 = s32[256]{0:T(256)S(1)} reshape(s32[8,32]{1,0:T(8,128)} %bitcast.1) | data formatting | bytes 2048 | tf_op jit(solution)/shard_map/reshape | solution.py:29
  1.4 0.3 convert_reduce_fusion
  1.7 0.2 select_reduce_fusion.1
  1.9 0.1 select_reduce_fusion
  2.0 0.1 select_reduce_fusion.2
  2.1 0.1 select_reduce_fusion.3
  2.2 0.1 pad_add_fusion.idx
  2.3 61.7 %soap_step.1 = (bf16[512,2048]{1,0:T(8,128)(2,1)S(1)}, bf16[16,8,256]{2,1,0:T(8,128)(2,1)S(1)}, f32[16,8,256]{2,1,0:T(8,128)S(1)}, f32[16,8,256]{2,1,0:T(8,128)S(1)}, f32[16,8,256]{2,1,0:T(8,128)S(1)}) custom-call(s32[96]{0:T(128)S(1)} %pad_add_fusion.idx, bf16[16,8,256]{2,1,0:T(8,128)(2,1)} %left_h.1, bf16[16,8,256]{2,1,0:T(8,128)(2,1)} %right_h.1, ...), custom_call_target="tpu_custom_call" | custom-call | flops 201326592 | bytes 6291456 | tf_op jit(solution)/shard_map/soap_step/pallas_call | solution.py:394
  64.0 1.6 %store.1 = (bf16[512,2048]{1,0:T(8,128)(2,1)}, bf16[16,8,256]{2,1,0:T(8,128)(2,1)}, f32[16,8,256]{2,1,0:T(8,128)}, f32[16,8,256]{2,1,0:T(8,128)}, f32[16,8,256]{2,1,0:T(8,128)}) custom-call(bf16[512,2048]{1,0:T(8,128)(2,1)S(1)} %get-tuple-element.10.refs_0_, bf16[16,8,256]{2,1,0:T(8,128)(2,1)S(1)} %get-tuple-element.11.refs_1_, ...), custom_call_target="tpu_custom_call" | custom-call | bytes 5242880 | tf_op jit(solution)/shard_map/store/pallas_call | solution.py:435
  (4 shorter events, 0.0 us)

commit v3 on v2

--- a/solution.py
+++ b/solution.py
@@ -19,29 +19,54 @@
 KEPT = 16
 W = 256
 PR, PC = 16, 128
-PARTS = 4
+PARTS = 2
 FAR_Y = (4, 3, 5, 2, 6, 1, 7, 0)
 FAR_Z = (2, 1, 3, 0)
 MESH = pl.DeviceIdType.MESH
 
 
-def routing(owner, here):
-    flat = owner.T.reshape(-1)
-    place = jnp.arange(flat.shape[0], dtype=jnp.int32)
-    ident = place % owner.shape[0] * owner.shape[1] + place // owner.shape[0]
-    source = ident // KEPT
-    same = (flat[:, None] == flat[None, :]) & (ident[None, :] < ident[:, None])
-    rank = jnp.sum(same.astype(jnp.int32), axis=1)
-    pair = jnp.sum((same & (source[:, None] == source[None, :])).astype(jnp.int32), axis=1)
-    local = jnp.arange(KEPT, dtype=jnp.int32)
-    slots = jnp.arange(SHARDS * CAP, dtype=jnp.int32)
-    mine = (ident[None, :] == here * KEPT + local[:, None]).astype(jnp.int32)
-    dest = jnp.sum(mine * (flat * CAP + pair)[None, :], axis=1)
-    owned = ((flat == here)[None, :] & (rank[None, :] == local[:, None])).astype(jnp.int32)
-    recv = jnp.sum(owned * (source * CAP + pair)[None, :], axis=1)
-    send_pick = jnp.sum((dest[None, :] == slots[:, None]).astype(jnp.int32) * local[None, :], axis=1)
-    back_pick = jnp.sum((recv[None, :] == slots[:, None]).astype(jnp.int32) * local[None, :], axis=1)
-    return jnp.concatenate([send_pick, recv, back_pick, dest])
+def routing(owner_t, here):
+    i32, f32 = jnp.int32, jnp.float32
+    count = owner_t.shape[0] * owner_t.shape[1]
+    cols, rows = owner_t.shape
+    square = lax.broadcasted_iota(i32, (rows, rows), 0) == lax.broadcasted_iota(i32, (rows, rows), 1)
+
+    def total(mask, value, axis):
+        return jnp.sum(jnp.where(mask, value, 0).astype(f32), axis=axis, keepdims=True).astype(i32)
+
+    def numbers(shape, axis):
+        at = lax.broadcasted_iota(i32, shape, axis)
+        return at % rows * cols + at // rows, at % rows * cols // KEPT
+
+    flat = jnp.concatenate([total(square, owner_t[j : j + 1, :], 1) for j in range(cols)], axis=0)
+    ident, source = numbers((count, 1), 0)
+    ident_r, source_r = numbers((1, count), 1)
+    diagonal = ident == ident_r
+    flat_r = total(diagonal, flat, 0)
+    same = (flat == flat_r) & (ident_r < ident)
+    rank = total(same, 1, 1)
+    pair = total(same & (source == source_r), 1, 1)
+    to_slot, from_slot = flat * CAP + pair, source * CAP + pair
+    lane = lax.broadcasted_iota(i32, (1, 128), 1)
+    slots = SHARDS * CAP
+    owned = flat == here
+    picked = jnp.where(
+        lane < slots,
+        jnp.where((source == here) & (to_slot == lane), ident - here * KEPT, 0),
+        jnp.where(
+            lane < slots + KEPT,
+            jnp.where(owned & (rank == lane - slots), from_slot, 0),
+            jnp.where(
+                lane < 2 * slots + KEPT,
+                jnp.where(owned & (from_slot == lane - slots - KEPT), rank, 0),
+                jnp.where(ident == here * KEPT + lane - 2 * slots - KEPT, to_slot, 0),
+            ),
+        ),
+    )
+    row = jnp.sum(picked.astype(f32), axis=0, keepdims=True).astype(i32)
+    of_slots = ((lane >= slots) & (lane < slots + KEPT)) | (lane >= 2 * slots + KEPT)
+    row = jnp.maximum(jnp.minimum(row, jnp.where(of_slots, slots - 1, KEPT - 1)), 0)
+    return jnp.broadcast_to(row, (8, 128))
 
 
 def fold(x):
@@ -71,12 +96,12 @@
 
 
 def kernel(
-    idx, left_h, right_h, avg_h, avg_sq_h, grad, left_gram_h, right_gram_h,
+    owner_h, left_h, right_h, avg_h, avg_sq_h, grad, left_gram_h, right_gram_h,
     update, new_avg, new_avg_sq, new_left, new_right,
-    left, right, avg, avg_sq, whole, left_gram, right_gram,
+    owner, table_v, table, left, right, avg, avg_sq, whole, left_gram, right_gram,
     folded, bases_out, moments_out, bases_in, moments_in, bases_row, moments_row, bases, moments,
     rsend, rbuf, grams, tsend, trecv,
-    load_sem, send_sem, recv_sem, z_send, ag_send, ag_recv,
+    load_sem, table_sem, send_sem, recv_sem, z_send, ag_send, ag_recv,
 ):
     r = lax.axis_index("rep")
     s = lax.axis_index("shard")
@@ -110,11 +135,14 @@
         pltpu.make_async_copy(src, dst, load_sem.at[n])
         for n, (src, dst) in enumerate(
             [(left_h, left), (right_h, right), (avg_h, avg), (avg_sq_h, avg_sq),
-             (grad, whole), (left_gram_h, left_gram), (right_gram_h, right_gram)]
+             (grad, whole), (left_gram_h, left_gram), (right_gram_h, right_gram), (owner_h, owner)]
         )
     ]
-    for copy in loads[:4]:
+    for copy in (loads[7], *loads[:4]):
         copy.start()
+
+    def idx(n):
+        return table[0, n]
 
     barrier = pltpu.get_barrier_semaphore()
     for peer in ss:
@@ -127,13 +155,20 @@
                 if t or v:
                     pl.semaphore_signal(barrier, inc=1, **to(ys[t] * ZS + zs[v]))
 
-    for n, ref in enumerate((left, right, avg, avg_sq)):
-        loads[n].wait()
-        folded[:, n] = fold(ref[...])
-    for n in range(SHARDS * CAP):
-        block = folded[idx[SHARDS * CAP + KEPT + n]]
-        bases_out[n] = block[:2]
-        moments_out[n] = block[2:]
+    loads[7].wait()
+    table_v[...] = routing(owner[...], s)
+    pltpu.make_async_copy(table_v, table, table_sem).start()
+
+    def pack(first, refs, out):
+        for n, ref in enumerate(refs):
+            loads[first + n].wait()
+            folded[:, n] = fold(ref[...])
+        if first == 0:
+            pltpu.make_async_copy(table_v, table, table_sem).wait()
+        for n in range(SHARDS * CAP):
+            out[n] = folded[idx(SHARDS * CAP + KEPT + n)]
+
+    pack(0, (left, right), bases_out)
     pl.semaphore_wait(barrier, jnp.where(is_hub, SHARDS - 1 + KEPT - 1, SHARDS - 1 + KEPT))
 
     mine = pl.ds(s * CAP, CAP)
@@ -146,8 +181,9 @@
             ).start()
 
     exchange(bases_out, bases_in, 0)
+    pack(2, (avg, avg_sq), moments_out)
     exchange(moments_out, moments_in, 1)
-    for copy in loads[4:]:
+    for copy in loads[4:7]:
         copy.start()
 
     def to_hub(src, dst, n):
@@ -175,18 +211,18 @@
     ):
         wait_bytes(got, recv_sem.at[n])
         for b in range(KEPT):
-            row[b] = got[idx[2 * SHARDS * CAP + KEPT + b]]
+            row[b] = got[idx(2 * SHARDS * CAP + KEPT + b)]
         to_hub(row, out, 2 + n)
 
     block_me = 2 * y + z_half
-    row_of = [pl.multiple_of(ys[t] // 4 * W, W) for t in range(YS)]
-    col_of = [pl.multiple_of(ys[t] % 4 * (2 * W), W) for t in range(YS)]
 
     @pl.when(is_hub)
     def _():
         loads[4].wait()
-        here = (pl.ds(row_of[0], W), pl.ds(pl.multiple_of(col_of[0] + z_half * W, W), W))
-        g = whole[here]
+        g = whole[
+            pl.ds(pl.multiple_of(y // 4 * W, W), W),
+            pl.ds(pl.multiple_of(y % 4 * (2 * W) + z_half * W, W), W),
+        ]
         wait_bytes(bases, recv_sem.at[2])
         lb = unfold(bases[:, 0]).reshape(W, W).astype(jnp.bfloat16)
         rb = unfold(bases[:, 1]).reshape(W, W).astype(jnp.bfloat16)
@@ -199,7 +235,7 @@
         second = BETA_TWO * v0 + (1.0 - BETA_TWO) * turned * turned
         scaled = (first / (jnp.sqrt(second) + EPSILON)).astype(jnp.bfloat16)
         back = nt(scaled, rb).astype(jnp.bfloat16)
-        update[here] = tn(lb, back).astype(jnp.bfloat16)
+        update[block_me] = tn(lb, back).astype(jnp.bfloat16)
         rsend[...] = fold(turned.reshape(REPS, 8, W))
 
     ups = (ys[1] * ZS + z, ys[7] * ZS + z)
@@ -209,10 +245,7 @@
     names = {}
 
     def region(t, bit, rows):
-        return update.at[
-            pl.ds(pl.multiple_of(row_of[t] + rows[0], 16), rows[1] - rows[0]),
-            pl.ds(pl.multiple_of(col_of[t] + bit * W, W), W),
-        ]
+        return update.at[2 * ys[t] + bit, pl.ds(rows[0], rows[1] - rows[0])]
 
     def push(ref, peer, key):
         n = names.setdefault(key, len(names))
@@ -282,6 +315,27 @@
                 v = jnp.where(z_odd == 1, v[8:], v[:8])
                 grams[b, n] = jnp.concatenate([v[:, :PC], v[:, PC:]], axis=0).astype(jnp.bfloat16)
 
+    def send_r(n):
+        @pl.when(is_hub)
+        def _():
+            t = FAR_Y[n]
+            for v in FAR_Z:
+                q = ys[t] * ZS + zs[v]
+                if t or v:
+                    pltpu.make_async_remote_copy(
+                        rsend.at[q], rbuf.at[block_me], send_sem.at[4], recv_sem.at[4], **to(q)
+                    ).start()
+                else:
+                    pltpu.make_async_copy(rsend.at[r], rbuf.at[block_me], recv_sem.at[4]).start()
+
+    def to_owners():
+        wait_bytes(rbuf, recv_sem.at[4])
+        for m in range(SHARDS * CAP):
+            b = idx(m)
+            tsend[m, 0] = rbuf[b]
+            tsend[m, 1:] = grams[b]
+        exchange(tsend, trecv, 5)
+
     def side(n):
         if n == 0:
 
@@ -289,36 +343,18 @@
             def _():
                 loads[4].wait()
 
-        if n < YS // 2:
-
-            @pl.when(is_hub)
-            def _():
-                for t in FAR_Y[2 * n : 2 * n + 2]:
-                    for v in FAR_Z:
-                        q = ys[t] * ZS + zs[v]
-                        if t or v:
-                            pltpu.make_async_remote_copy(
-                                rsend.at[q], rbuf.at[block_me], send_sem.at[4], recv_sem.at[4], **to(q)
-                            ).start()
-                        else:
-                            pltpu.make_async_copy(rsend.at[r], rbuf.at[block_me], recv_sem.at[4]).start()
-
-        if n < KEPT // 2:
+        if n < YS:
+            send_r(n)
             gram_rows((2 * n, 2 * n + 1))
-        elif n == KEPT // 2:
-            wait_bytes(rbuf, recv_sem.at[4])
-            for m in range(SHARDS * CAP):
-                b = idx[m]
-                tsend[m, 0] = rbuf[b]
-                tsend[m, 1:] = grams[b]
-            exchange(tsend, trecv, 5)
+        elif n == YS:
+            to_owners()
 
     def own_rows():
         wait_bytes(trecv, recv_sem.at[5])
-        for copy in loads[5:]:
+        for copy in loads[5:7]:
             copy.wait()
         for n in range(KEPT):
-            turned, gl, gr = unfold(trecv[idx[SHARDS * CAP + n]])
+            turned, gl, gr = unfold(trecv[idx(SHARDS * CAP + n)])
             new_avg[n] = (BETA_ONE * avg[n].astype(jnp.float32) + (1.0 - BETA_ONE) * turned).astype(jnp.bfloat16)
             new_avg_sq[n] = BETA_TWO * avg_sq[n] + (1.0 - BETA_TWO) * turned * turned
             new_left[n] = BETA_TWO * left_gram[n] + (1.0 - BETA_TWO) * gl
@@ -330,12 +366,11 @@
     order += [(y_step, 1, m, 1) for m in range(PARTS)]
     for d in (2, 3, 4):
         order += [(y_step, c, m, d) for c in range(2) for m in range(PARTS)]
-    count = 0
-    for step, *args in order[:-2]:
+    first = 2 * PARTS - 1
+    for count, (step, *args) in enumerate(order[:-2]):
         step(*args)
-        if count <= KEPT // 2:
-            side(count)
-        count += 1
+        if first <= count <= first + YS:
+            side(count - first)
         if count == len(order) - 4:
             own_rows()
 
@@ -367,11 +402,13 @@
     copies = []
     for n in range(count):
         src, dst = refs[n], refs[count + n]
-        parts = 8 if n == 0 else 1
-        size = src.shape[0] // parts
-        for p in range(parts):
-            rows = pl.ds(p * size, size)
-            copies.append(pltpu.make_async_copy(src.at[rows], dst.at[rows], sems.at[len(copies)]))
+        if n == 0:
+            for b in range(KEPT):
+                i, j = b // 8, b % 8
+                place = dst.at[i * W : (i + 1) * W, j * W : (j + 1) * W]
+                copies.append(pltpu.make_async_copy(src.at[b], place, sems.at[len(copies)]))
+        else:
+            copies.append(pltpu.make_async_copy(src, dst, sems.at[len(copies)]))
     for copy in copies:
         copy.start()
     for copy in copies:
@@ -379,8 +416,6 @@
 
 
 def body(grad, owner, left_basis, right_basis, avg, avg_sq, left_gram, right_gram):
-    here = lax.axis_index("shard")
-    idx = routing(owner, here)
     vmem = pl.BlockSpec(memory_space=pltpu.VMEM)
     hbm = pl.BlockSpec(memory_space=pltpu.HBM)
     bf16, f32 = jnp.bfloat16, jnp.float32
@@ -389,14 +424,17 @@
     outs = [jax.ShapeDtypeStruct(x.shape, x.dtype) for x in (grad, avg, avg_sq, left_gram, right_gram)]
     operands = [
         pltpu.with_memory_space_constraint(x, pltpu.HBM)
-        for x in (left_basis, right_basis, avg, avg_sq, grad, left_gram, right_gram)
+        for x in (owner.T, left_basis, right_basis, avg, avg_sq, grad, left_gram, right_gram)
     ]
     results = pl.pallas_call(
         kernel,
-        out_shape=outs,
-        in_specs=[pl.BlockSpec(memory_space=pltpu.SMEM)] + [hbm] * 7,
+        out_shape=[jax.ShapeDtypeStruct((KEPT, W, W), bf16)] + outs[1:],
+        in_specs=[hbm] * 8,
         out_specs=[vmem] * 5,
         scratch_shapes=[
+            pltpu.VMEM(owner.shape[::-1], jnp.int32),
+            pltpu.VMEM((8, 128), jnp.int32),
+            pltpu.SMEM((8, 128), jnp.int32),
             pltpu.VMEM(rows, bf16),
             pltpu.VMEM(rows, bf16),
             pltpu.VMEM(rows, bf16),
@@ -404,7 +442,7 @@
             pltpu.VMEM(grad.shape, bf16),
             pltpu.VMEM(rows, f32),
             pltpu.VMEM(rows, f32),
-            pltpu.VMEM((KEPT, 4, PR, PC), bf16),
+            pltpu.VMEM((KEPT, 2, PR, PC), bf16),
             pltpu.VMEM((slots, 2, PR, PC), bf16),
             pltpu.VMEM((slots, 2, PR, PC), bf16),
             pltpu.VMEM((slots, 2, PR, PC), bf16),
@@ -418,7 +456,8 @@
             pltpu.VMEM((KEPT, 2, PR, PC), bf16),
             pltpu.VMEM((slots, 3, PR, PC), bf16),
             pltpu.VMEM((slots, 3, PR, PC), bf16),
-            pltpu.SemaphoreType.DMA((7,)),
+            pltpu.SemaphoreType.DMA((8,)),
+            pltpu.SemaphoreType.DMA,
             pltpu.SemaphoreType.DMA((6,)),
             pltpu.SemaphoreType.DMA((6,)),
             pltpu.SemaphoreType.DMA((3 * PARTS,)),
@@ -430,14 +469,14 @@
         ),
         cost_estimate=pl.CostEstimate(flops=12 * W**3, bytes_accessed=6 << 20, transcendentals=0),
         name="soap_step",
-    )(idx, *operands)
+    )(*operands)
     return tuple(
         pl.pallas_call(
             store_kernel,
             out_shape=outs,
             in_specs=[pl.BlockSpec(memory_space=pl.ANY)] * 5,
             out_specs=[hbm] * 5,
-            scratch_shapes=[pltpu.SemaphoreType.DMA((12,))],
+            scratch_shapes=[pltpu.SemaphoreType.DMA((KEPT + 4,))],
             compiler_params=pltpu.CompilerParams(vmem_limit_bytes=4 * 1024 * 1024),
             cost_estimate=pl.CostEstimate(flops=0, bytes_accessed=5 << 20, transcendentals=0),
             name="store",

time: 65.9 us -> 67.1 us (1.018)
  the two profiles are of different devices: /device:TPU:6 before, /device:TPU:4 now
where the time goes in v3:
time: 67.1 us; the launch traced here: 67 us
  Pallas kernels  66.4 us (99%)
    pallas_call x1, Pallas kernels, body(): pl.pallas_call(kernel, out_shape=[jax.ShapeDtypeStruct((KEPT, W, W), bf16...  64.7 us
    pallas_call x1, Pallas kernels, body(): pl.pallas_call(store_kernel, out_shape=outs, in_specs=[pl.BlockSpec(memor...  1.63 us

profile of v3, /device:TPU:4, one launch (start us, length us, event | category | flops | bytes accessed | tf_op | source)
XLA Modules:
  0.0 67.0 jit_solution(2590870397161019301)
XLA Ops:
  0.6 64.7 %soap_step.1 = (bf16[16,256,256]{2,1,0:T(8,128)(2,1)S(1)}, bf16[16,8,256]{2,1,0:T(8,128)(2,1)S(1)}, f32[16,8,256]{2,1,0:T(8,128)S(1)}, f32[16,8,256]{2,1,0:T(8,128)S(1)}, f32[16,8,256]{2,1,0:T(8,128)S(1)}) custom-call(s32[8,32]{1,0:T(8,128)} %bitcast.1, bf16[16,8,256]{2,1,0:T(8,128)(2,1)} %left_h.1, bf16[16,8,256]{2,1,0:T(8,128)(2,1)} %right_h.1, ...), custom_call_target="tpu_custom_call" | custom-call | flops 201326592 | bytes 6291456 | tf_op jit(solution)/shard_map/soap_step/pallas_call | solution.py:429
  65.4 1.6 %store.1 = (bf16[512,2048]{1,0:T(8,128)(2,1)}, bf16[16,8,256]{2,1,0:T(8,128)(2,1)}, f32[16,8,256]{2,1,0:T(8,128)}, f32[16,8,256]{2,1,0:T(8,128)}, f32[16,8,256]{2,1,0:T(8,128)}) custom-call(bf16[16,256,256]{2,1,0:T(8,128)(2,1)S(1)} %get-tuple-element.10.refs_0_, bf16[16,8,256]{2,1,0:T(8,128)(2,1)S(1)} %get-tuple-element.11.refs_1_, ...), custom_call_target="tpu_custom_call" | custom-call | bytes 5242880 | tf_op jit(solution)/shard_map/store/pallas_call | solution.py:474

commit v4 on v3

--- a/solution.py
+++ b/solution.py
@@ -186,6 +186,23 @@
     for copy in loads[4:7]:
         copy.start()
 
+    strip_at = pl.multiple_of(PR * (2 * y + z_half), PR)
+    picks = (
+        lax.broadcasted_iota(jnp.int32, (PR, W), 1)
+        == lax.broadcasted_iota(jnp.int32, (PR, W), 0) + strip_at
+    ).astype(jnp.float32).astype(jnp.bfloat16)
+
+    def gram_rows(blocks):
+        for b in blocks:
+            i, j = b // 8, b % 8
+            g = whole[i * W : (i + 1) * W, j * W : (j + 1) * W]
+            strip = whole[pl.ds(i * W + strip_at, PR), j * W : (j + 1) * W]
+            both = nt(jnp.concatenate([strip, picks], axis=0), g)
+            wide = nn(both[PR:].astype(jnp.bfloat16), g)
+            for n, v in enumerate((both[:PR], wide)):
+                v = jnp.where(z_odd == 1, v[8:], v[:8])
+                grams[b, n] = jnp.concatenate([v[:, :PC], v[:, PC:]], axis=0).astype(jnp.bfloat16)
+
     def to_hub(src, dst, n):
         for t in FAR_Y:
             p = p0 if t % 2 == 0 else 1 - p0
@@ -206,6 +223,8 @@
                 else:
                     remote()
 
+    loads[4].wait()
+    gram_rows(range(0, 6))
     for n, (got, row, out) in enumerate(
         ((bases_in, bases_row, bases), (moments_in, moments_row, moments))
     ):
@@ -213,12 +232,12 @@
         for b in range(KEPT):
             row[b] = got[idx(2 * SHARDS * CAP + KEPT + b)]
         to_hub(row, out, 2 + n)
+        gram_rows(range(6, 10) if n == 0 else range(10, KEPT))
 
     block_me = 2 * y + z_half
 
     @pl.when(is_hub)
     def _():
-        loads[4].wait()
         g = whole[
             pl.ds(pl.multiple_of(y // 4 * W, W), W),
             pl.ds(pl.multiple_of(y % 4 * (2 * W) + z_half * W, W), W),
@@ -298,35 +317,18 @@
             if d < YS // 2:
                 y_push(c, m, d + 1, way)
 
-    strip_at = pl.multiple_of(PR * (2 * y + z_half), PR)
-    picks = (
-        lax.broadcasted_iota(jnp.int32, (PR, W), 1)
-        == lax.broadcasted_iota(jnp.int32, (PR, W), 0) + strip_at
-    ).astype(jnp.float32).astype(jnp.bfloat16)
-
-    def gram_rows(blocks):
-        for b in blocks:
-            i, j = b // 8, b % 8
-            g = whole[i * W : (i + 1) * W, j * W : (j + 1) * W]
-            strip = whole[pl.ds(i * W + strip_at, PR), j * W : (j + 1) * W]
-            both = nt(jnp.concatenate([strip, picks], axis=0), g)
-            wide = nn(both[PR:].astype(jnp.bfloat16), g)
-            for n, v in enumerate((both[:PR], wide)):
-                v = jnp.where(z_odd == 1, v[8:], v[:8])
-                grams[b, n] = jnp.concatenate([v[:, :PC], v[:, PC:]], axis=0).astype(jnp.bfloat16)
-
-    def send_r(n):
+    def send_r():
         @pl.when(is_hub)
         def _():
-            t = FAR_Y[n]
-            for v in FAR_Z:
-                q = ys[t] * ZS + zs[v]
-                if t or v:
-                    pltpu.make_async_remote_copy(
-                        rsend.at[q], rbuf.at[block_me], send_sem.at[4], recv_sem.at[4], **to(q)
-                    ).start()
-                else:
-                    pltpu.make_async_copy(rsend.at[r], rbuf.at[block_me], recv_sem.at[4]).start()
+            for t in FAR_Y:
+                for v in FAR_Z:
+                    q = ys[t] * ZS + zs[v]
+                    if t or v:
+                        pltpu.make_async_remote_copy(
+                            rsend.at[q], rbuf.at[block_me], send_sem.at[4], recv_sem.at[4], **to(q)
+                        ).start()
+                    else:
+                        pltpu.make_async_copy(rsend.at[r], rbuf.at[block_me], recv_sem.at[4]).start()
 
     def to_owners():
         wait_bytes(rbuf, recv_sem.at[4])
@@ -335,19 +337,6 @@
             tsend[m, 0] = rbuf[b]
             tsend[m, 1:] = grams[b]
         exchange(tsend, trecv, 5)
-
-    def side(n):
-        if n == 0:
-
-            @pl.when(jnp.logical_not(is_hub))
-            def _():
-                loads[4].wait()
-
-        if n < YS:
-            send_r(n)
-            gram_rows((2 * n, 2 * n + 1))
-        elif n == YS:
-            to_owners()
 
     def own_rows():
         wait_bytes(trecv, recv_sem.at[5])
@@ -366,11 +355,12 @@
     order += [(y_step, 1, m, 1) for m in range(PARTS)]
     for d in (2, 3, 4):
         order += [(y_step, c, m, d) for c in range(2) for m in range(PARTS)]
-    first = 2 * PARTS - 1
     for count, (step, *args) in enumerate(order[:-2]):
         step(*args)
-        if first <= count <= first + YS:
-            side(count - first)
+        if count == PARTS - 1:
+            send_r()
+        if count == 4 * PARTS:
+            to_owners()
         if count == len(order) - 4:
             own_rows()
 

time: 67.1 us -> 63.3 us (0.943)
  the two profiles are of different devices: /device:TPU:4 before, /device:TPU:6 now
where the time goes in v4:
time: 63.3 us; the launch traced here: 62.8 us
  Pallas kernels  62.2 us (98%)
  between operations  0.64 us (1%)
    pallas_call x1, Pallas kernels, body(): pl.pallas_call(kernel, out_shape=[jax.ShapeDtypeStruct((KEPT, W, W), bf16...  60.5 us
    pallas_call x1, Pallas kernels, body(): pl.pallas_call(store_kernel, out_shape=outs, in_specs=[pl.BlockSpec(memor...  1.63 us

profile of v4, /device:TPU:6, one launch (start us, length us, event | category | flops | bytes accessed | tf_op | source)
XLA Modules:
  0.0 62.8 jit_solution(9344443772622808888)
XLA Ops:
  0.6 60.5 %soap_step.1 = (bf16[16,256,256]{2,1,0:T(8,128)(2,1)S(1)}, bf16[16,8,256]{2,1,0:T(8,128)(2,1)S(1)}, f32[16,8,256]{2,1,0:T(8,128)S(1)}, f32[16,8,256]{2,1,0:T(8,128)S(1)}, f32[16,8,256]{2,1,0:T(8,128)S(1)}) custom-call(s32[8,32]{1,0:T(8,128)} %bitcast.1, bf16[16,8,256]{2,1,0:T(8,128)(2,1)} %left_h.1, bf16[16,8,256]{2,1,0:T(8,128)(2,1)} %right_h.1, ...), custom_call_target="tpu_custom_call" | custom-call | flops 201326592 | bytes 6291456 | tf_op jit(solution)/shard_map/soap_step/pallas_call | solution.py:419
  61.2 1.6 %store.1 = (bf16[512,2048]{1,0:T(8,128)(2,1)}, bf16[16,8,256]{2,1,0:T(8,128)(2,1)}, f32[16,8,256]{2,1,0:T(8,128)}, f32[16,8,256]{2,1,0:T(8,128)}, f32[16,8,256]{2,1,0:T(8,128)}) custom-call(bf16[16,256,256]{2,1,0:T(8,128)(2,1)S(1)} %get-tuple-element.10.refs_0_, bf16[16,8,256]{2,1,0:T(8,128)(2,1)S(1)} %get-tuple-element.11.refs_1_, ...), custom_call_target="tpu_custom_call" | custom-call | bytes 5242880 | tf_op jit(solution)/shard_map/store/pallas_call | solution.py:464

commit v5 on v4

--- a/solution.py
+++ b/solution.py
@@ -117,13 +117,14 @@
     zs = [wrap(z + t, ZS) for t in range(ZS)]
     z_low, x, core = s // 8, s % 8 // 2, s % 2
     xs = [wrap(x + t, 4) for t in range(4)]
+    moves = (
+        (1, 2, 1), (1, 2, 0), (0, 2, 1), (0, 2, 0), (1, 1, 1), (1, 1, 0), (1, 3, 1), (1, 3, 0),
+        (0, 1, 1), (0, 1, 0), (0, 3, 1), (0, 3, 0), (1, 0, 1), (1, 0, 0), (0, 0, 1),
+    )
     ss = [
-        (1 - z_low if a else z_low) * 8 + xs[b] * 2 + (1 - core if c else core)
-        for a, b, c in (
-            (1, 2, 1), (1, 2, 0), (0, 2, 1), (0, 2, 0), (1, 1, 1), (1, 1, 0), (1, 3, 1), (1, 3, 0),
-            (0, 1, 1), (0, 1, 0), (0, 3, 1), (0, 3, 0), (1, 0, 1), (1, 0, 0), (0, 0, 1),
-        )
+        (1 - z_low if a else z_low) * 8 + xs[b] * 2 + (1 - core if c else core) for a, b, c in moves
     ]
+    r_out = y * ZS + jnp.where(z_low == 1, zs[1], zs[3])
 
     def to(rep):
         return dict(device_id={"rep": rep}, device_id_type=MESH)
@@ -145,8 +146,13 @@
         return table[0, n]
 
     barrier = pltpu.get_barrier_semaphore()
-    for peer in ss:
+    def outside(peer):
+        return dict(device_id={"rep": r_out, "shard": peer}, device_id_type=MESH)
+
+    for peer, move in zip(ss, moves):
         pl.semaphore_signal(barrier, inc=1, **over(peer))
+        if move[0]:
+            pl.semaphore_signal(barrier, inc=1, **outside(peer))
 
     @pl.when(is_hub)
     def _():
@@ -169,20 +175,21 @@
             out[n] = folded[idx(SHARDS * CAP + KEPT + n)]
 
     pack(0, (left, right), bases_out)
-    pl.semaphore_wait(barrier, jnp.where(is_hub, SHARDS - 1 + KEPT - 1, SHARDS - 1 + KEPT))
+    pl.semaphore_wait(barrier, jnp.where(is_hub, SHARDS - 1 + 8 + KEPT - 1, SHARDS - 1 + 8 + KEPT))
 
     mine = pl.ds(s * CAP, CAP)
 
-    def exchange(src, dst, n):
+    def exchange(src, dst, n, turned=False):
         pltpu.make_async_copy(src.at[mine], dst.at[mine], recv_sem.at[n]).start()
-        for peer in ss:
+        for peer, move in zip(ss, moves):
             pltpu.make_async_remote_copy(
-                src.at[pl.ds(peer * CAP, CAP)], dst.at[mine], send_sem.at[n], recv_sem.at[n], **over(peer)
+                src.at[pl.ds(peer * CAP, CAP)], dst.at[mine], send_sem.at[n], recv_sem.at[n],
+                **(outside(peer) if turned and move[0] else over(peer)),
             ).start()
 
     exchange(bases_out, bases_in, 0)
     pack(2, (avg, avg_sq), moments_out)
-    exchange(moments_out, moments_in, 1)
+    exchange(moments_out, moments_in, 1, turned=True)
     for copy in loads[4:7]:
         copy.start()
 
@@ -248,8 +255,17 @@
         half = nn(lb, g).astype(jnp.bfloat16)
         turned = nn(half, rb)
         wait_bytes(moments, recv_sem.at[3])
-        m0 = unfold(moments[:, 0]).reshape(W, W)
-        v0 = unfold(moments[:, 1]).reshape(W, W)
+        crossed = idx(2 * SHARDS * CAP + KEPT + block_me) // (8 * CAP) != z_low
+
+        def in_order(x):
+            x = unfold(x).reshape(YS, ZS, 8, W)
+            up = jnp.concatenate([x[:, ZS - 1 :], x[:, : ZS - 1]], axis=1)
+            down = jnp.concatenate([x[:, 1:], x[:, :1]], axis=1)
+            x = jnp.where(crossed, jnp.where(z_low == 1, up, down), x)
+            return x.reshape(W, W)
+
+        m0 = in_order(moments[:, 0])
+        v0 = in_order(moments[:, 1])
         first = BETA_ONE * m0 + (1.0 - BETA_ONE) * turned
         second = BETA_TWO * v0 + (1.0 - BETA_TWO) * turned * turned
         scaled = (first / (jnp.sqrt(second) + EPSILON)).astype(jnp.bfloat16)

time: 63.3 us -> 64.2 us (1.014)
  the two profiles are of different devices: /device:TPU:6 before, /device:TPU:64 now
where the time goes in v5:
time: 64.2 us; the launch traced here: 64 us
  Pallas kernels  63.4 us (99%)
    pallas_call x1, Pallas kernels, body(): pl.pallas_call(kernel, out_shape=[jax.ShapeDtypeStruct((KEPT, W, W), bf16...  61.8 us
    pallas_call x1, Pallas kernels, body(): pl.pallas_call(store_kernel, out_shape=outs, in_specs=[pl.BlockSpec(memor...  1.63 us

profile of v5, /device:TPU:64, one launch (start us, length us, event | category | flops | bytes accessed | tf_op | source)
XLA Modules:
  0.0 64.0 jit_solution(10825537727069691226)
XLA Ops:
  0.6 61.8 %soap_step.1 = (bf16[16,256,256]{2,1,0:T(8,128)(2,1)S(1)}, bf16[16,8,256]{2,1,0:T(8,128)(2,1)S(1)}, f32[16,8,256]{2,1,0:T(8,128)S(1)}, f32[16,8,256]{2,1,0:T(8,128)S(1)}, f32[16,8,256]{2,1,0:T(8,128)S(1)}) custom-call(s32[8,32]{1,0:T(8,128)} %bitcast.1, bf16[16,8,256]{2,1,0:T(8,128)(2,1)} %left_h.1, bf16[16,8,256]{2,1,0:T(8,128)(2,1)} %right_h.1, ...), custom_call_target="tpu_custom_call" | custom-call | flops 201326592 | bytes 6291456 | tf_op jit(solution)/shard_map/soap_step/pallas_call | solution.py:435
  62.4 1.6 %store.1 = (bf16[512,2048]{1,0:T(8,128)(2,1)}, bf16[16,8,256]{2,1,0:T(8,128)(2,1)}, f32[16,8,256]{2,1,0:T(8,128)}, f32[16,8,256]{2,1,0:T(8,128)}, f32[16,8,256]{2,1,0:T(8,128)}) custom-call(bf16[16,256,256]{2,1,0:T(8,128)(2,1)S(1)} %get-tuple-element.10.refs_0_, bf16[16,8,256]{2,1,0:T(8,128)(2,1)S(1)} %get-tuple-element.11.refs_1_, ...), custom_call_target="tpu_custom_call" | custom-call | bytes 5242880 | tf_op jit(solution)/shard_map/store/pallas_call | solution.py:480

commit v6 on v4

--- a/solution.py
+++ b/solution.py
@@ -100,7 +100,7 @@
     update, new_avg, new_avg_sq, new_left, new_right,
     owner, table_v, table, left, right, avg, avg_sq, whole, left_gram, right_gram,
     folded, bases_out, moments_out, bases_in, moments_in, bases_row, moments_row, bases, moments,
-    rsend, rbuf, grams, tsend, trecv,
+    rsend, rbuf, grams, tsend, trecv, r_send, r_recv,
     load_sem, table_sem, send_sem, recv_sem, z_send, ag_send, ag_recv,
 ):
     r = lax.axis_index("rep")
@@ -224,7 +224,7 @@
                     remote()
 
     loads[4].wait()
-    gram_rows(range(0, 6))
+    gram_rows(range(0, 4))
     for n, (got, row, out) in enumerate(
         ((bases_in, bases_row, bases), (moments_in, moments_row, moments))
     ):
@@ -232,7 +232,16 @@
         for b in range(KEPT):
             row[b] = got[idx(2 * SHARDS * CAP + KEPT + b)]
         to_hub(row, out, 2 + n)
-        gram_rows(range(6, 10) if n == 0 else range(10, KEPT))
+        if n == 0:
+            gram_rows(range(4, 9))
+
+    def grams_to_owners():
+        gram_rows(range(9, KEPT))
+        for m in range(SHARDS * CAP):
+            tsend[m] = grams[idx(m)]
+        exchange(tsend, trecv, 5)
+
+    pl.when(jnp.logical_not(is_hub))(grams_to_owners)
 
     block_me = 2 * y + z_half
 
@@ -333,17 +342,18 @@
     def to_owners():
         wait_bytes(rbuf, recv_sem.at[4])
         for m in range(SHARDS * CAP):
-            b = idx(m)
-            tsend[m, 0] = rbuf[b]
-            tsend[m, 1:] = grams[b]
-        exchange(tsend, trecv, 5)
+            r_send[m] = rbuf[idx(m)]
+        exchange(r_send, r_recv, 6)
 
     def own_rows():
         wait_bytes(trecv, recv_sem.at[5])
+        wait_bytes(r_recv, recv_sem.at[6])
         for copy in loads[5:7]:
             copy.wait()
         for n in range(KEPT):
-            turned, gl, gr = unfold(trecv[idx(SHARDS * CAP + n)])
+            at = idx(SHARDS * CAP + n)
+            gl, gr = unfold(trecv[at])
+            turned = unfold(r_recv[pl.ds(at, 1)])[0]
             new_avg[n] = (BETA_ONE * avg[n].astype(jnp.float32) + (1.0 - BETA_ONE) * turned).astype(jnp.bfloat16)
             new_avg_sq[n] = BETA_TWO * avg_sq[n] + (1.0 - BETA_TWO) * turned * turned
             new_left[n] = BETA_TWO * left_gram[n] + (1.0 - BETA_TWO) * gl
@@ -359,6 +369,7 @@
         step(*args)
         if count == PARTS - 1:
             send_r()
+            pl.when(is_hub)(grams_to_owners)
         if count == 4 * PARTS:
             to_owners()
         if count == len(order) - 4:
@@ -366,7 +377,7 @@
 
     for copy in pending:
         copy.wait_send()
-    for n, ref in ((0, bases_out), (1, moments_out), (5, tsend)):
+    for n, ref in ((0, bases_out), (1, moments_out), (5, tsend), (6, r_send)):
         wait_bytes(ref.at[pl.ds(0, CAP * (SHARDS - 1))], send_sem.at[n])
 
     @pl.when(is_hub)
@@ -444,12 +455,14 @@
             pltpu.VMEM((REPS, PR, PC), bf16),
             pltpu.VMEM((KEPT, PR, PC), bf16),
             pltpu.VMEM((KEPT, 2, PR, PC), bf16),
-            pltpu.VMEM((slots, 3, PR, PC), bf16),
-            pltpu.VMEM((slots, 3, PR, PC), bf16),
+            pltpu.VMEM((slots, 2, PR, PC), bf16),
+            pltpu.VMEM((slots, 2, PR, PC), bf16),
+            pltpu.VMEM((slots, PR, PC), bf16),
+            pltpu.VMEM((slots, PR, PC), bf16),
             pltpu.SemaphoreType.DMA((8,)),
             pltpu.SemaphoreType.DMA,
-            pltpu.SemaphoreType.DMA((6,)),
-            pltpu.SemaphoreType.DMA((6,)),
+            pltpu.SemaphoreType.DMA((7,)),
+            pltpu.SemaphoreType.DMA((7,)),
             pltpu.SemaphoreType.DMA((3 * PARTS,)),
             pltpu.SemaphoreType.DMA((18 * PARTS,)),
             pltpu.SemaphoreType.DMA((18 * PARTS,)),

time: 63.3 us -> 63.3 us (level)
  no operation moved by 1% of the time
where the time goes in v6:
time: 63.3 us; the launch traced here: 63.1 us
  Pallas kernels  62.5 us (99%)
  between operations  0.64 us (1%)
    pallas_call x1, Pallas kernels, body(): pl.pallas_call(kernel, out_shape=[jax.ShapeDtypeStruct((KEPT, W, W), bf16...  60.8 us
    pallas_call x1, Pallas kernels, body(): pl.pallas_call(store_kernel, out_shape=outs, in_specs=[pl.BlockSpec(memor...  1.63 us

profile of v6, /device:TPU:6, one launch (start us, length us, event | category | flops | bytes accessed | tf_op | source)
XLA Modules:
  0.0 63.1 jit_solution(15277670833960084233)
XLA Ops:
  0.6 60.8 %soap_step.1 = (bf16[16,256,256]{2,1,0:T(8,128)(2,1)S(1)}, bf16[16,8,256]{2,1,0:T(8,128)(2,1)S(1)}, f32[16,8,256]{2,1,0:T(8,128)S(1)}, f32[16,8,256]{2,1,0:T(8,128)S(1)}, f32[16,8,256]{2,1,0:T(8,128)S(1)}) custom-call(s32[8,32]{1,0:T(8,128)} %bitcast.1, bf16[16,8,256]{2,1,0:T(8,128)(2,1)} %left_h.1, bf16[16,8,256]{2,1,0:T(8,128)(2,1)} %right_h.1, ...), custom_call_target="tpu_custom_call" | custom-call | flops 201326592 | bytes 6291456 | tf_op jit(solution)/shard_map/soap_step/pallas_call | solution.py:430
  61.5 1.6 %store.1 = (bf16[512,2048]{1,0:T(8,128)(2,1)}, bf16[16,8,256]{2,1,0:T(8,128)(2,1)}, f32[16,8,256]{2,1,0:T(8,128)}, f32[16,8,256]{2,1,0:T(8,128)}, f32[16,8,256]{2,1,0:T(8,128)}) custom-call(bf16[16,256,256]{2,1,0:T(8,128)(2,1)S(1)} %get-tuple-element.10.refs_0_, bf16[16,8,256]{2,1,0:T(8,128)(2,1)S(1)} %get-tuple-element.11.refs_1_, ...), custom_call_target="tpu_custom_call" | custom-call | bytes 5242880 | tf_op jit(solution)/shard_map/store/pallas_call | solution.py:477

commit v7 on v6

--- a/solution.py
+++ b/solution.py
@@ -362,9 +362,8 @@
     order = [(z_step, 0, m) for m in range(PARTS)]
     for m in range(PARTS):
         order += [(z_step, 1, m), (y_step, 0, m, 1)]
-    order += [(y_step, 1, m, 1) for m in range(PARTS)]
-    for d in (2, 3, 4):
-        order += [(y_step, c, m, d) for c in range(2) for m in range(PARTS)]
+    for c, d in ((0, 2), (1, 1), (0, 3), (1, 2), (0, 4), (1, 3), (1, 4)):
+        order += [(y_step, c, m, d) for m in range(PARTS)]
     for count, (step, *args) in enumerate(order[:-2]):
         step(*args)
         if count == PARTS - 1:

time: 63.3 us -> 66 us (1.043)
  Pallas kernels: 62.5 us -> 65.2 us
    pallas_call x1, Pallas kernels: 60.8 us -> 63.6 us  [body(): pl.pallas_call(kernel, out_shape=[jax.ShapeDtypeStruct((KEPT, W, W), bf16...]
where the time goes in v7:
time: 66 us; the launch traced here: 65.9 us
  Pallas kernels  65.2 us (99%)
    pallas_call x1, Pallas kernels, body(): pl.pallas_call(kernel, out_shape=[jax.ShapeDtypeStruct((KEPT, W, W), bf16...  63.6 us
    pallas_call x1, Pallas kernels, body(): pl.pallas_call(store_kernel, out_shape=outs, in_specs=[pl.BlockSpec(memor...  1.63 us

profile of v7, /device:TPU:6, one launch (start us, length us, event | category | flops | bytes accessed | tf_op | source)
XLA Modules:
  0.0 65.9 jit_solution(18248123602378158115)
XLA Ops:
  0.6 63.6 %soap_step.1 = (bf16[16,256,256]{2,1,0:T(8,128)(2,1)S(1)}, bf16[16,8,256]{2,1,0:T(8,128)(2,1)S(1)}, f32[16,8,256]{2,1,0:T(8,128)S(1)}, f32[16,8,256]{2,1,0:T(8,128)S(1)}, f32[16,8,256]{2,1,0:T(8,128)S(1)}) custom-call(s32[8,32]{1,0:T(8,128)} %bitcast.1, bf16[16,8,256]{2,1,0:T(8,128)(2,1)} %left_h.1, bf16[16,8,256]{2,1,0:T(8,128)(2,1)} %right_h.1, ...), custom_call_target="tpu_custom_call" | custom-call | flops 201326592 | bytes 6291456 | tf_op jit(solution)/shard_map/soap_step/pallas_call | solution.py:429
  64.2 1.6 %store.1 = (bf16[512,2048]{1,0:T(8,128)(2,1)}, bf16[16,8,256]{2,1,0:T(8,128)(2,1)}, f32[16,8,256]{2,1,0:T(8,128)}, f32[16,8,256]{2,1,0:T(8,128)}, f32[16,8,256]{2,1,0:T(8,128)}) custom-call(bf16[16,256,256]{2,1,0:T(8,128)(2,1)S(1)} %get-tuple-element.10.refs_0_, bf16[16,8,256]{2,1,0:T(8,128)(2,1)S(1)} %get-tuple-element.11.refs_1_, ...), custom_call_target="tpu_custom_call" | custom-call | bytes 5242880 | tf_op jit(solution)/shard_map/store/pallas_call | solution.py:476

commit v8 on v6

--- a/solution.py
+++ b/solution.py
@@ -19,7 +19,7 @@
 KEPT = 16
 W = 256
 PR, PC = 16, 128
-PARTS = 2
+PARTS = 4
 FAR_Y = (4, 3, 5, 2, 6, 1, 7, 0)
 FAR_Z = (2, 1, 3, 0)
 MESH = pl.DeviceIdType.MESH

time: 63.3 us -> 63.3 us (level)
  no operation moved by 1% of the time
where the time goes in v8:
time: 63.3 us; the launch traced here: 63.1 us
  Pallas kernels  62.4 us (99%)
  between operations  0.64 us (1%)
    pallas_call x1, Pallas kernels, body(): pl.pallas_call(kernel, out_shape=[jax.ShapeDtypeStruct((KEPT, W, W), bf16...  60.8 us
    pallas_call x1, Pallas kernels, body(): pl.pallas_call(store_kernel, out_shape=outs, in_specs=[pl.BlockSpec(memor...  1.63 us

profile of v8, /device:TPU:6, one launch (start us, length us, event | category | flops | bytes accessed | tf_op | source)
XLA Modules:
  0.0 63.1 jit_solution(15951018932280236392)
XLA Ops:
  0.6 60.8 %soap_step.1 = (bf16[16,256,256]{2,1,0:T(8,128)(2,1)S(1)}, bf16[16,8,256]{2,1,0:T(8,128)(2,1)S(1)}, f32[16,8,256]{2,1,0:T(8,128)S(1)}, f32[16,8,256]{2,1,0:T(8,128)S(1)}, f32[16,8,256]{2,1,0:T(8,128)S(1)}) custom-call(s32[8,32]{1,0:T(8,128)} %bitcast.1, bf16[16,8,256]{2,1,0:T(8,128)(2,1)} %left_h.1, bf16[16,8,256]{2,1,0:T(8,128)(2,1)} %right_h.1, ...), custom_call_target="tpu_custom_call" | custom-call | flops 201326592 | bytes 6291456 | tf_op jit(solution)/shard_map/soap_step/pallas_call | solution.py:430
  61.4 1.6 %store.1 = (bf16[512,2048]{1,0:T(8,128)(2,1)}, bf16[16,8,256]{2,1,0:T(8,128)(2,1)}, f32[16,8,256]{2,1,0:T(8,128)}, f32[16,8,256]{2,1,0:T(8,128)}, f32[16,8,256]{2,1,0:T(8,128)}) custom-call(bf16[16,256,256]{2,1,0:T(8,128)(2,1)S(1)} %get-tuple-element.10.refs_0_, bf16[16,8,256]{2,1,0:T(8,128)(2,1)S(1)} %get-tuple-element.11.refs_1_, ...), custom_call_target="tpu_custom_call" | custom-call | bytes 5242880 | tf_op jit(solution)/shard_map/store/pallas_call | solution.py:477

commit v9 on v6

--- a/solution.py
+++ b/solution.py
@@ -289,9 +289,9 @@
 
     @pl.when(is_hub)
     def _():
-        for m, rows in enumerate(parts):
-            ref = region(0, bits[0], rows)
-            for n, (c, peer) in enumerate(((1, zs[2]), (1, z_next), (0, z_pair))):
+        for n, (c, peer) in enumerate(((1, zs[2]), (1, z_next), (0, z_pair))):
+            for m, rows in enumerate(parts):
+                ref = region(0, bits[0], rows)
                 key = names.setdefault(("z", c, m), len(names))
                 pltpu.make_async_remote_copy(
                     ref, ref, z_send.at[3 * m + n], ag_recv.at[key], **to(y * ZS + peer)
@@ -364,7 +364,7 @@
         order += [(z_step, 1, m), (y_step, 0, m, 1)]
     order += [(y_step, 1, m, 1) for m in range(PARTS)]
     for d in (2, 3, 4):
-        order += [(y_step, c, m, d) for c in range(2) for m in range(PARTS)]
+        order += [(y_step, c, m, d) for c in (1, 0) for m in range(PARTS)]
     for count, (step, *args) in enumerate(order[:-2]):
         step(*args)
         if count == PARTS - 1:

time: 63.3 us -> 65.4 us (1.033)
  Pallas kernels: 62.5 us -> 64.6 us
    pallas_call x1, Pallas kernels: 60.8 us -> 63 us  [body(): pl.pallas_call(kernel, out_shape=[jax.ShapeDtypeStruct((KEPT, W, W), bf16...]
where the time goes in v9:
time: 65.4 us; the launch traced here: 65.3 us
  Pallas kernels  64.6 us (99%)
    pallas_call x1, Pallas kernels, body(): pl.pallas_call(kernel, out_shape=[jax.ShapeDtypeStruct((KEPT, W, W), bf16...  63 us
    pallas_call x1, Pallas kernels, body(): pl.pallas_call(store_kernel, out_shape=outs, in_specs=[pl.BlockSpec(memor...  1.63 us

profile of v9, /device:TPU:6, one launch (start us, length us, event | category | flops | bytes accessed | tf_op | source)
XLA Modules:
  0.0 65.3 jit_solution(12385356520582980317)
XLA Ops:
  0.6 63.0 %soap_step.1 = (bf16[16,256,256]{2,1,0:T(8,128)(2,1)S(1)}, bf16[16,8,256]{2,1,0:T(8,128)(2,1)S(1)}, f32[16,8,256]{2,1,0:T(8,128)S(1)}, f32[16,8,256]{2,1,0:T(8,128)S(1)}, f32[16,8,256]{2,1,0:T(8,128)S(1)}) custom-call(s32[8,32]{1,0:T(8,128)} %bitcast.1, bf16[16,8,256]{2,1,0:T(8,128)(2,1)} %left_h.1, bf16[16,8,256]{2,1,0:T(8,128)(2,1)} %right_h.1, ...), custom_call_target="tpu_custom_call" | custom-call | flops 201326592 | bytes 6291456 | tf_op jit(solution)/shard_map/soap_step/pallas_call | solution.py:430
  63.6 1.6 %store.1 = (bf16[512,2048]{1,0:T(8,128)(2,1)}, bf16[16,8,256]{2,1,0:T(8,128)(2,1)}, f32[16,8,256]{2,1,0:T(8,128)}, f32[16,8,256]{2,1,0:T(8,128)}, f32[16,8,256]{2,1,0:T(8,128)}) custom-call(bf16[16,256,256]{2,1,0:T(8,128)(2,1)S(1)} %get-tuple-element.10.refs_0_, bf16[16,8,256]{2,1,0:T(8,128)(2,1)S(1)} %get-tuple-element.11.refs_1_, ...), custom_call_target="tpu_custom_call" | custom-call | bytes 5242880 | tf_op jit(solution)/shard_map/store/pallas_call | solution.py:477
